TPU v7x, 256 devices: a whole 4x4x8 slice. The times are simulated.
256 devices in a mesh: row: 16 (over y_lo, x, core), col: 16 (over y_hi, z).
Axes of the slice: x: 4, y: 4 (y_hi: 2, y_lo: 2; y = y_hi * 2 + y_lo), z: 8, core: 2. Of those that a mesh axis runs over, the one named last changes fastest.
Arguments:
- pair: float32 [384, 384, 128], P('row', 'col'), may hold values from -6 to 6
- grad_out: float32 [384, 384, 128], P('row', 'col'), may hold values from -6 to 6
- w_in_out: bfloat16 [128, 384], replicated, may hold values from -0.5 to 0.5
- w_out_out: bfloat16 [64, 128], replicated, may hold values from -0.75 to 0.75
- w_in_in: bfloat16 [128, 384], replicated, may hold values from -0.5 to 0.5
- w_out_in: bfloat16 [64, 128], replicated, may hold values from -0.75 to 0.75
Outputs:
- pair_new: float32 [384, 384, 128], P('row', 'col')
- pair_grad: float32 [384, 384, 128], P('row', 'col')
- grad_win_out: float32 [128, 384], replicated
- grad_wout_out: float32 [64, 128], replicated
- grad_win_in: float32 [128, 384], replicated
- grad_wout_in: float32 [64, 128], replicated
All inputs are finite; a program needn't handle non-finite values.
Results may differ from a plain program's by a relative error of at most 0.035.
Values may be sent and summed in bfloat16 or wider, within the bound.
No kernel may reach another device: no remote copies, remote signals or barrier semaphores. Data moves between devices by JAX's collectives and lax.ppermute only.
A program may use at most 64 MiB of HBM per device.

v0:
```python
import jax
import jax.numpy as jnp
from jax import lax
from jax.sharding import PartitionSpec as P

C = 128


EPS = 1e-05
HIGH = lax.Precision.HIGHEST


def layer_norm(values):
    center = values - jnp.mean(values, axis=-1, keepdims=True)
    spread = jnp.mean(center * center, axis=-1, keepdims=True)
    return center * lax.rsqrt(spread + EPS)


def gating(projected):
    hidden = (projected.shape[-1] - C) // 4
    left = (jax.nn.sigmoid(projected[..., hidden : 2 * hidden]) * projected[..., :hidden]).astype(
        jnp.bfloat16
    )
    right = (
        jax.nn.sigmoid(projected[..., 3 * hidden : 4 * hidden])
        * projected[..., 2 * hidden : 3 * hidden]
    ).astype(jnp.bfloat16)
    gate = jax.nn.sigmoid(projected[..., 4 * hidden :])
    return (left, right, gate)


def prepare(pair, w_in):
    normed = layer_norm(pair).astype(jnp.bfloat16)
    projected = jnp.dot(normed, w_in, preferred_element_type=jnp.float32)
    return (normed, projected)


def finish(mixed, pair, gate, w_out):
    post = layer_norm(mixed).astype(jnp.bfloat16)
    return pair + gate * jnp.dot(post, w_out, preferred_element_type=jnp.float32)


def finish_back(grad_new, mixed, gate, w_out):
    post = layer_norm(mixed).astype(jnp.bfloat16)
    projected_out = jnp.dot(post, w_out, preferred_element_type=jnp.float32)
    grad_gate = grad_new * projected_out
    grad_proj = grad_new * gate
    grad_w = jnp.dot(
        post.reshape(-1, w_out.shape[0]).astype(jnp.float32).T,
        grad_proj.reshape(-1, w_out.shape[1]),
        precision=HIGH,
    )
    grad_post = jnp.dot(grad_proj, w_out.astype(jnp.float32).T, precision=HIGH)
    _, pull = jax.vjp(layer_norm, mixed)
    return (pull(grad_post)[0], grad_gate, grad_w)


def prepare_back(pair, normed, projected, grad_left, grad_right, grad_gate, w_in):
    _, pull = jax.vjp(gating, projected)
    grad_projected = pull((grad_left, grad_right, grad_gate))[0]
    width = grad_projected.shape[-1]
    grad_w = jnp.dot(
        normed.reshape(-1, w_in.shape[0]).astype(jnp.float32).T,
        grad_projected.reshape(-1, width),
        precision=HIGH,
    )
    grad_normed = jnp.dot(grad_projected, w_in.astype(jnp.float32).T, precision=HIGH)
    _, pull_norm = jax.vjp(layer_norm, pair)
    return (pull_norm(grad_normed)[0], grad_w)


def local(pair, grad_out, w_in_out, w_out_out, w_in_in, w_out_in):
    row_count = lax.axis_size("row")
    row_len = pair.shape[0]
    normed_one, projected_one = prepare(pair, w_in_out)
    left_one, right_one, gate_one = gating(projected_one)
    right_every = lax.all_gather(right_one, "row", axis=0, tiled=True)
    piece = right_every
    mixed_one = jnp.transpose(
        lax.psum_scatter(
            jnp.einsum("ikh,jkh->jih", left_one, piece, preferred_element_type=jnp.float32).astype(
                jnp.bfloat16
            ),
            "col",
            scatter_dimension=0,
            tiled=True,
        ).astype(jnp.float32),
        (1, 0, 2),
    )
    pair_mid = finish(mixed_one, pair, gate_one, w_out_out)
    normed_two, projected_two = prepare(pair_mid, w_in_in)
    left_two, right_two, gate_two = gating(projected_two)
    left_every = lax.all_gather(left_two, "col", axis=1, tiled=True)
    piece = left_every
    mixed_two = lax.psum_scatter(
        jnp.einsum("kih,kjh->ijh", piece, right_two, preferred_element_type=jnp.float32).astype(
            jnp.bfloat16
        ),
        "row",
        scatter_dimension=0,
        tiled=True,
    ).astype(jnp.float32)
    pair_new = finish(mixed_two, pair_mid, gate_two, w_out_in)
    grad_mixed_two, grad_gate_two, grad_wout_in = finish_back(
        grad_out, mixed_two, gate_two, w_out_in
    )
    grad_bf_two = grad_mixed_two.astype(jnp.bfloat16)
    grad_every = lax.all_gather(grad_bf_two, "row", axis=0, tiled=True)
    piece = grad_every
    grad_left_two = jnp.transpose(
        lax.psum_scatter(
            jnp.einsum("kjh,ijh->ikh", right_two, piece, preferred_element_type=jnp.float32).astype(
                jnp.bfloat16
            ),
            "col",
            scatter_dimension=0,
            tiled=True,
        ).astype(jnp.float32),
        (1, 0, 2),
    )
    grad_right_two = jnp.einsum(
        "kih,ijh->kjh", left_every, grad_every, preferred_element_type=jnp.float32
    )
    grad_low_two, grad_win_in = prepare_back(
        pair_mid,
        normed_two,
        projected_two,
        grad_left_two.astype(jnp.bfloat16),
        grad_right_two.astype(jnp.bfloat16),
        grad_gate_two,
        w_in_in,
    )
    grad_mid = grad_out + grad_low_two
    grad_win_in, grad_wout_in = lax.psum((grad_win_in, grad_wout_in), ("row", "col"))
    grad_mixed_one, grad_gate_one, grad_wout_out = finish_back(
        grad_mid, mixed_one, gate_one, w_out_out
    )
    grad_bf_one = grad_mixed_one.astype(jnp.bfloat16)
    grad_rows = lax.all_gather(grad_bf_one, "col", axis=1, tiled=True)
    piece = grad_rows
    grad_right_one = lax.psum_scatter(
        jnp.einsum("ijh,ikh->jkh", piece, left_one, preferred_element_type=jnp.float32).astype(
            jnp.bfloat16
        ),
        "row",
        scatter_dimension=0,
        tiled=True,
    )
    grad_left_one = jnp.einsum(
        "ijh,jkh->ikh", grad_rows, right_every, preferred_element_type=jnp.float32
    )
    grad_low_one, grad_win_out = prepare_back(
        pair,
        normed_one,
        projected_one,
        grad_left_one.astype(jnp.bfloat16),
        grad_right_one,
        grad_gate_one,
        w_in_out,
    )
    pair_grad = grad_mid + grad_low_one
    grad_win_out, grad_wout_out = lax.psum((grad_win_out, grad_wout_out), ("row", "col"))
    scale = 1.0 / (row_len * row_count)
    return (
        pair_new,
        pair_grad,
        grad_win_out * scale,
        grad_wout_out * scale,
        grad_win_in * scale,
        grad_wout_in * scale,
    )


def solution(mesh):
    placed = (P("row", "col", None), P("row", "col", None), P(), P(), P(), P())
    return jax.shard_map(
        local,
        mesh=mesh,
        in_specs=placed,
        out_specs=(P("row", "col", None), P("row", "col", None), P(), P(), P(), P()),
        check_vma=False,
    )
```

profile of v0, /device:TPU:1, one launch (start us, length us, event | category | flops | bytes accessed | tf_op | source)
XLA Modules:
  0.0 1372.0 jit_solution(14438631105631338528)
XLA Ops:
  7.2 1.1 reduce_sum.140
  8.4 1.2 multiply_reduce_fusion.3
  9.6 1.4 fusion.62
  11.0 0.9 multiply_convert_fusion.3
  11.9 1.0 copy.204
  12.9 40.1 %all-gather.5.cloned.1.call-done = bf16[384,24,64]{2,1,0:T(8,128)(2,1)} async-done(((bf16[24,24,64]{2,1,0:T(8,128)(2,1)}), bf16[384,24,64]{2,1,0:T(8,128)(2,1)}) %all-gather.5.cloned.1.call-update) | async-done | bytes 1179664 | tf_op jit(solution)/shard_map/all_gather | solution.py:77
  53.1 3.5 copy.207
  56.6 1.6 fusion
  58.2 2.8 copy.184
  61.1 207.0 %reduce-scatter.7.cloned.1.call-done = bf16[24,24,64]{2,1,0:T(8,128)(2,1)} async-done(((bf16[384,24,64]{2,1,0:T(8,128)(2,1)}), bf16[24,24,64]{2,1,0:T(8,128)(2,1)}) %reduce-scatter.7.cloned.1.call-update) | async-done | bytes 73744 | tf_op jit(solution)/shard_map/reduce_scatter | solution.py:80
  268.1 1.1 bitcast_reduce_fusion
  269.2 1.2 fusion.39
  270.4 2.0 fusion.84
  272.4 0.3 multiply_reduce_fusion.2
  272.8 0.6 copy-done.20
  273.3 0.4 fusion.59
  273.7 0.9 multiply_convert_fusion
  274.7 1.0 copy.201
  275.6 85.2 %all-gather.7.cloned.1.call-done = bf16[24,384,64]{2,1,0:T(8,128)(2,1)} async-done(((bf16[24,24,64]{2,1,0:T(8,128)(2,1)}), bf16[24,384,64]{2,1,0:T(8,128)(2,1)}) %all-gather.7.cloned.1.call-update) | async-done | bytes 1179664 | tf_op jit(solution)/shard_map/all_gather | solution.py:93
  360.9 3.9 copy.187
  364.8 3.1 fusion.1
  367.9 4.2 copy.188
  372.1 63.0 %reduce-scatter.9.cloned.1.call-done = bf16[24,24,64]{2,1,0:T(8,128)(2,1)} async-done(((bf16[384,24,64]{2,1,0:T(8,128)(2,1)}), bf16[24,24,64]{2,1,0:T(8,128)(2,1)}) %reduce-scatter.9.cloned.1.call-update) | async-done | bytes 73744 | tf_op jit(solution)/shard_map/reduce_scatter | solution.py:95
  435.2 1.1 convert_reduce_fusion
  436.3 1.4 fusion.10
  437.8 0.4 fusion.50
  438.4 1.0 add_convert_fusion.1
  439.5 39.2 %all-gather.9.cloned.1.call-done = bf16[384,24,64]{2,1,0:T(8,128)(2,1)} async-done(((bf16[24,24,64]{2,1,0:T(8,128)(2,1)}), bf16[384,24,64]{2,1,0:T(8,128)(2,1)}) %all-gather.9.cloned.1.call-update) | async-done | bytes 1179664 | tf_op jit(solution)/shard_map/all_gather | solution.py:108
  478.7 10.7 copy.200
  489.4 7.2 fusion.3
  496.6 4.3 copy.210
  500.9 4.2 reshape.124
  505.4 2.3 fusion.12
  507.7 5.4 fusion.85
  513.1 1.9 copy.199
  515.0 188.8 %reduce-scatter.13.cloned.1.call-done = bf16[24,1536]{1,0:T(8,128)(2,1)} async-done(((bf16[384,1536]{1,0:T(8,128)(2,1)}), bf16[24,1536]{1,0:T(8,128)(2,1)}) %reduce-scatter.13.cloned.1.call-update) | async-done | bytes 73744
  703.9 1.0 reshape.125
  704.9 1.2 bitcast_multiply_fusion.5
  706.2 0.8 multiply_reduce_fusion.1
  707.2 0.4 fusion.66
  707.7 1.1 fusion.15
  708.8 0.4 fusion.41
  709.5 0.4 fusion.51
  710.0 0.4 add_convert_fusion
  710.3 0.7 copy.203
  711.1 2.2 convolution_bitcast_fusion.2
  713.3 1.2 convolution_bitcast_fusion.3
  714.6 83.8 %all-gather.11.cloned.1.call-done = bf16[24,384,64]{2,0,1:T(8,128)(2,1)} async-done(((bf16[24,24,64]{2,0,1:T(8,128)(2,1)}), bf16[24,384,64]{2,0,1:T(8,128)(2,1)}) %all-gather.11.cloned.1.call-update) | async-done | bytes 1179664 | tf_op jit(solution)/shard_map/all_gather | solution.py:139
  798.3 3.5 copy.205
  801.8 2.6 fusion.2
  804.5 4.2 copy.206
  809.0 3.2 convolution_bitcast_fusion
  812.1 232.3 %all-reduce.15.cloned.1.call-done = (f32[64,128]{1,0:T(8,128)}, f32[64,128]{1,0:T(8,128)}) async-done(((f32[64,128]{1,0:T(8,128)}, f32[64,128]{1,0:T(8,128)}), (f32[64,128]{1,0:T(8,128)}, f32[64,128]{1,0:T(8,128)})) %all-reduce.15.cloned.1.call-update) | async-done | bytes 65552 | tf_op jit(solution)/shard_map/psum | solution.py:162
  1044.4 1.4 broadcast_multiply_fusion.2
  1045.8 1.4 fusion.86
  1047.2 1.3 copy.209
  1048.5 57.6 %reduce-scatter.11.cloned.1.call-done = bf16[24,24,64]{2,1,0:T(8,128)(2,1)} async-done(((bf16[384,24,64]{2,1,0:T(8,128)(2,1)}), bf16[24,24,64]{2,1,0:T(8,128)(2,1)}) %reduce-scatter.11.cloned.1.call-update) | async-done | bytes 73744 | tf_op jit(solution)/shard_map/reduce_scatter | solution.py:141
  1106.1 1.2 convert_multiply_fusion.1
  1107.3 1.7 convolution_bitcast_fusion.1
  1109.1 0.8 multiply_reduce_fusion
  1109.9 0.4 fusion.67
  1110.4 1.1 add_add_fusion.4
  1111.5 251.9 %all-reduce.17.cloned.1.call-done = (f32[128,384]{1,0:T(8,128)}, f32[128,384]{1,0:T(8,128)}) async-done(((f32[128,384]{1,0:T(8,128)}, f32[128,384]{1,0:T(8,128)}), (f32[128,384]{1,0:T(8,128)}, f32[128,384]{1,0:T(8,128)})) %all-reduce.17.cloned.1.call-update) | async-done | bytes 393232 | tf_op jit(solution)/shard_map/psum | solution.py:162
  1363.4 1.8 broadcast_multiply_fusion
  (100 shorter events, 1.8 us)
Async XLA Ops:
  7.2 266.2 %copy-start = (bf16[128,384]{1,0:T(8,128)(2,1)S(1)}, bf16[128,384]{1,0:T(8,128)(2,1)}, u32[]{:S(2)}) copy-start(bf16[128,384]{1,0:T(8,128)(2,1)} %param.10) | copy-start | bytes 294916
  7.2 45.9 %all-gather.5.cloned.1.call-start = ((), (), s32[]{:S(2)}) async-start(), calls=%async_computation.4 | async-start | bytes 2506752 | tf_op jit(solution)/shard_map/all_gather | solution.py:77
  9.6 2.3 copy-start.18
  11.9 256.2 %reduce-scatter.7.cloned.1.call-start = ((), (), s32[]{:S(2)}) async-start(), calls=%async_computation.5 | async-start | bytes 2506752 | tf_op jit(solution)/shard_map/reduce_scatter | solution.py:80
  61.0 209.4 %copy-start.2 = (f32[24,24,128]{2,1,0:T(8,128)S(1)}, f32[24,24,128]{2,1,0:T(8,128)}, u32[]{:S(2)}) copy-start(f32[24,24,128]{2,1,0:T(8,128)} %param.6) | copy-start | bytes 884740
  61.0 209.4 %copy-start.30 = (bf16[64,128]{1,0:T(8,128)(2,1)S(1)}, bf16[64,128]{1,0:T(8,128)(2,1)}, u32[]{:S(2)}) copy-start(bf16[64,128]{1,0:T(8,128)(2,1)} %param.9) | copy-start | bytes 49156
  61.1 299.8 %all-gather.7.cloned.1.call-start = ((), (), s32[]{:S(2)}) async-start(), calls=%async_computation.6 | async-start | bytes 2506752 | tf_op jit(solution)/shard_map/all_gather | solution.py:93
  270.4 2.0 copy-start.22
  270.4 2.0 copy-start.24
  272.4 435.2 %copy-start.4 = (f32[24,24,128]{2,1,0:T(8,128)}, f32[24,24,128]{2,1,0:T(8,128)S(1)}, u32[]{:S(2)}) copy-start(f32[24,24,128]{2,1,0:T(8,128)S(1)} %get-tuple-element.21) | copy-start | bytes 884740
  272.7 0.6 copy-start.20
  274.6 160.5 %reduce-scatter.9.cloned.1.call-start = ((), (), s32[]{:S(2)}) async-start(), calls=%async_computation.7 | async-start | bytes 2506752 | tf_op jit(solution)/shard_map/reduce_scatter | solution.py:95
  372.1 106.6 %all-gather.9.cloned.1.call-start = ((), (), s32[]{:S(2)}) async-start(), calls=%async_computation.8 | async-start | bytes 2506752 | tf_op jit(solution)/shard_map/all_gather | solution.py:108
  435.2 2.6 copy-start.6
  436.3 1.9 copy-start.27
  437.8 0.6 copy-start.28
  439.4 264.4 %reduce-scatter.13.cloned.1.call-start = ((), (), s32[]{:S(2)}) async-start(), calls=%async_computation.11 | async-start | bytes 1253376
  505.1 293.2 %all-gather.11.cloned.1.call-start = ((), (), s32[]{:S(2)}) async-start(), calls=%async_computation.9 | async-start | bytes 2506752 | tf_op jit(solution)/shard_map/all_gather | solution.py:139
  505.4 2.3 copy-start.1
  704.9 1.3 copy-start.32
  706.2 0.9 copy-start.14
  706.2 0.9 copy-start.15
  706.2 0.9 copy-start.16
  706.2 1.0 copy-start.17
  706.2 0.9 copy-start.21
  706.2 1.4 copy-start.11
  706.2 1.4 copy-start.12
  707.6 1.2 copy-start.5
  707.6 1.2 copy-start.31
  708.8 1.6 copy-start.8
  708.8 0.7 copy-start.23
  708.8 0.8 copy-start.25
  709.2 1.9 copy-start.7
  711.0 2.3 copy-start.26
  711.0 333.4 %all-reduce.15.cloned.1.call-start = ((), (), s32[]{:S(2)}) async-start(), calls=%async_computation.12 | async-start | bytes 131072 | tf_op jit(solution)/shard_map/psum | solution.py:162
  711.1 2.2 copy-start.9
  714.5 391.6 %reduce-scatter.11.cloned.1.call-start = ((), (), s32[]{:S(2)}) async-start(), calls=%async_computation.10 | async-start | bytes 2506752 | tf_op jit(solution)/shard_map/reduce_scatter | solution.py:141
  808.7 554.7 %all-reduce.17.cloned.1.call-start = ((), (), s32[]{:S(2)}) async-start(), calls=%async_computation.13 | async-start | bytes 786432 | tf_op jit(solution)/shard_map/psum | solution.py:162
  1048.5 58.8 %copy-start.3 = (f32[24,24,128]{2,1,0:T(8,128)S(1)}, f32[24,24,128]{2,1,0:T(8,128)}, u32[]{:S(2)}) copy-start(f32[24,24,128]{2,1,0:T(8,128)} %param.6) | copy-start | bytes 884740
  1048.5 58.8 %copy-start.13 = (f32[24,24,128]{2,1,0:T(8,128)S(1)}, f32[24,24,128]{2,1,0:T(8,128)}, u32[]{:S(2)}) copy-start(f32[24,24,128]{2,1,0:T(8,128)} %get-tuple-element.18) | copy-start | bytes 884740
  1107.3 1.8 copy-start.29
  1109.1 0.8 copy-start.19
  1109.1 1.3 copy-start.10
Sparse Core Ops, SparseCore 0:
  12.0 41.0 all-gather.4
  61.2 206.9 reduce-scatter.6
  274.7 86.0 all-gather.6
  372.2 62.8 reduce-scatter.8
  439.6 39.1 all-gather.8
  505.3 198.5 reduce-scatter.12
  711.2 87.0 all-gather.10
  805.5 238.8 all-reduce.14
  1047.1 58.9 reduce-scatter.10
  1113.0 250.2 all-reduce.16
where the time goes:
time: 1370 us
  waiting for transfers between devices  1250 us (91%)
  local copies, waits for them, and re-layouts  49.6 us (4%)
  matrix products  39 us (3%)
  other arithmetic  18.6 us (1%)
  between operations  14.8 us (1%)
    psum x2, waiting for transfers between devices, local(): lax.psum((grad_win_out, grad_wout_out), ('row', 'col'))  484 us
    reduce_scatter x1, waiting for transfers between devices, local(): lax.psum_scatter(jnp.einsum('ikh,jkh->jih', left_one, piece, preferred_el...  207 us
    unnamed x11, waiting for transfers between devices  189 us
    all_gather x1, waiting for transfers between devices, local(): left_every = lax.all_gather(left_two, 'col', axis=1, tiled=True)  85.2 us
    all_gather x1, waiting for transfers between devices, local(): grad_rows = lax.all_gather(grad_bf_one, 'col', axis=1, tiled=True)  83.8 us
    reduce_scatter x1, waiting for transfers between devices, local(): lax.psum_scatter(jnp.einsum('kih,kjh->ijh', piece, right_two, preferred_e...  63 us
    reduce_scatter x1, waiting for transfers between devices, local(): lax.psum_scatter(jnp.einsum('ijh,ikh->jkh', piece, left_one, preferred_el...  57.6 us
    all_gather x1, waiting for transfers between devices, local(): right_every = lax.all_gather(right_one, 'row', axis=0, tiled=True)  40.1 us
  transfers between devices with their start and end apart: 10, of which 10 were waited for; matrix products, arithmetic and copies ran while one was open for 2% of the time, Pallas kernels for 0%

commit v1 on v0

v1 whole, which is shorter than its diff:
```python
import functools

import jax
import jax.numpy as jnp
import numpy as np
from jax import lax
from jax.experimental import pallas as pl
from jax.experimental.pallas import tpu as pltpu
from jax.sharding import Mesh
from jax.sharding import PartitionSpec as P

EPS = 1e-05
F32 = jnp.float32
BF16 = jnp.bfloat16
PARTS = 4
ROW = ("row_hi", "row_lo")
COL = ("col_hi", "col_lo")


def dot(a, b, ca, cb):
    return lax.dot_general(a, b, (((ca,), (cb,)), ((), ())), preferred_element_type=F32)


def norm(x):
    center = x - jnp.mean(x, axis=0, keepdims=True)
    rstd = lax.rsqrt(jnp.mean(center * center, axis=0, keepdims=True) + EPS)
    return center * rstd, rstd


def norm_back(grad, normed, rstd):
    return rstd * (
        grad
        - jnp.mean(grad, axis=0, keepdims=True)
        - normed * jnp.mean(grad * normed, axis=0, keepdims=True)
    )


def swap_cells(ref, n):
    return jnp.concatenate([ref[pl.ds(j, n, stride=n), :] for j in range(n)], axis=0)


def project(x, w_in, proj_ref, left_ref, right_ref):
    h = left_ref.shape[0]
    normed, _ = norm(x)
    proj = dot(w_in, normed.astype(BF16), 0, 0)
    proj_ref[...] = proj
    left_ref[...] = (jax.nn.sigmoid(proj[h : 2 * h]) * proj[:h]).astype(BF16)
    right_ref[...] = (jax.nn.sigmoid(proj[3 * h : 4 * h]) * proj[2 * h : 3 * h]).astype(BF16)


def project_back(x, proj_ref, w_in, gl, gr, grad_gate, grad_w_ref):
    h = gl.shape[0]
    normed, rstd = norm(x)
    sa = jax.nn.sigmoid(proj_ref[h : 2 * h, :])
    sb = jax.nn.sigmoid(proj_ref[3 * h : 4 * h, :])
    gate = jax.nn.sigmoid(proj_ref[4 * h :, :])
    gla, grb = gl * sa, gr * sb
    grad = jnp.concatenate(
        [
            gla,
            gla * proj_ref[:h, :] * (1 - sa),
            grb,
            grb * proj_ref[2 * h : 3 * h, :] * (1 - sb),
            grad_gate * gate * (1 - gate),
        ],
        axis=0,
    ).astype(BF16)
    low = normed.astype(BF16)
    c = x.shape[0]
    for at in range(0, grad.shape[0], c):
        grad_w_ref[at : at + c, :] = dot(low, grad[at : at + c], 1, 1)
    return norm_back(dot(w_in, grad, 1, 0), normed, rstd)


def finish(mixed, w_out):
    normed, rstd = norm(mixed)
    post = normed.astype(BF16)
    return dot(w_out, post, 0, 0), normed, rstd, post


def finish_back(grad_new, gate, out, normed, rstd, post, w_out):
    grad_gate = grad_new * out
    grad_proj = (grad_new * gate).astype(BF16)
    grad_w = dot(post, grad_proj, 1, 1)
    return norm_back(dot(w_out, grad_proj, 1, 0), normed, rstd), grad_gate, grad_w


def summed(lo_ref, hi_ref):
    def total(ref):
        parts = [ref[q].astype(F32) for q in range(PARTS)]
        return (parts[0] + parts[1]) + (parts[2] + parts[3])

    return jnp.concatenate([total(lo_ref), total(hi_ref)], axis=1)


def start_one(pair_ref, w_ref, left_ref, right_ref, proj_ref, pair_t_ref):
    x = pair_ref[...].T
    pair_t_ref[...] = x
    project(x, w_ref[...], proj_ref, left_ref, right_ref)


def middle(
    lo_ref, hi_ref, pair_t_ref, proj1_ref, w_out_ref, w_in_ref,
    left_ref, right_ref, proj2_ref, mixed_ref, mid_ref, scratch,
):
    h = left_ref.shape[0]
    mixed = summed(lo_ref, hi_ref)
    mixed_ref[...] = mixed
    out, *_ = finish(mixed, w_out_ref[...])
    mid = pair_t_ref[...] + jax.nn.sigmoid(proj1_ref[4 * h :, :]) * out
    scratch[...] = mid.T
    mid = swap_cells(scratch, int(round(scratch.shape[0] ** 0.5))).T
    mid_ref[...] = mid
    project(mid, w_in_ref[...], proj2_ref, left_ref, right_ref)


def turn(
    lo_ref, hi_ref, mid_ref, proj_ref, grad_out_ref, w_out_ref,
    new_ref, grad_ref, grad_gate_ref, grad_w_ref, scratch,
):
    h = grad_ref.shape[0]
    n = new_ref.shape[0]
    out, normed, rstd, post = finish(summed(lo_ref, hi_ref), w_out_ref[...])
    gate = jax.nn.sigmoid(proj_ref[4 * h :, :])
    new = (mid_ref[...] + gate * out).T
    scratch[...] = new
    new_ref[...] = swap_cells(scratch, n).reshape(new_ref.shape)
    grad_new = swap_cells(grad_out_ref, n).T
    grad, grad_gate, grad_w = finish_back(grad_new, gate, out, normed, rstd, post, w_out_ref[...])
    grad_ref[...] = grad.astype(BF16)
    grad_gate_ref[...] = grad_gate
    grad_w_ref[...] = grad_w


def between(
    gl_ref, gr_ref, mid_ref, proj2_ref, grad_gate2_ref, w_in_ref, grad_out_ref, mixed_ref, proj1_ref, w_out_ref,
    grad_ref, grad_gate_ref, grad_mid_ref, grad_win_ref, grad_wout_ref, scratch,
):
    h = grad_ref.shape[0]
    low = project_back(
        mid_ref[...], proj2_ref, w_in_ref[...], gl_ref[...].astype(F32), gr_ref[...].astype(F32),
        grad_gate2_ref[...], grad_win_ref,
    )
    scratch[...] = low.T
    n = int(round(scratch.shape[0] ** 0.5))
    grad_mid = (grad_out_ref[...] + swap_cells(scratch, n)).T
    grad_mid_ref[...] = grad_mid
    w_out = w_out_ref[...]
    out, normed, rstd, post = finish(mixed_ref[...], w_out)
    gate = jax.nn.sigmoid(proj1_ref[4 * h :, :])
    grad, grad_gate, grad_w = finish_back(grad_mid, gate, out, normed, rstd, post, w_out)
    grad_ref[...] = grad.astype(BF16)
    grad_gate_ref[...] = grad_gate
    grad_wout_ref[...] = grad_w


def last(
    gl_ref, gr_ref, pair_t_ref, proj_ref, grad_gate_ref, w_in_ref, grad_mid_ref, win2_ref, wout2_ref, wout1_ref,
    pair_grad_ref, weights_ref, scratch,
):
    low = project_back(
        pair_t_ref[...], proj_ref, w_in_ref[...], gl_ref[...].astype(F32), gr_ref[...].astype(F32),
        grad_gate_ref[...], scratch,
    )
    pair_grad_ref[...] = (grad_mid_ref[...] + low).T
    weights_ref[...] = jnp.concatenate(
        [scratch[...], wout1_ref[...], win2_ref[...], wout2_ref[...]], axis=0
    ).astype(BF16)


def blocks(x, outer, inner, size, wide):
    rows = []
    for r in range(inner):
        rows.append(
            jnp.concatenate(
                [x[o * size : (o + 1) * size, r * wide : (r + 1) * wide] for o in range(outer)], axis=1
            )
        )
    return jnp.concatenate(rows, axis=0)


def reorder(ref, outer, inner):
    return jnp.concatenate([ref[pl.ds(r, outer, stride=inner), :] for r in range(inner)], axis=0)


def multiply(size, wide, first_ref, second_ref, lo_ref, hi_ref, first_out_ref, second_out_ref, scratch):
    part = first_ref.shape[0] // size
    first = blocks(first_ref[...].astype(F32), part, wide, size, wide).astype(BF16)
    scratch[...] = blocks(second_ref[...].astype(F32), part, wide, size, wide)
    second = reorder(scratch, wide, size).astype(BF16)
    first_out_ref[...] = first
    second_out_ref[...] = second
    out = blocks(dot(first, second, 1, 1), wide, size, size, wide).astype(BF16)
    half = lo_ref.shape[1]
    lo_ref[...] = out[:, :half]
    hi_ref[...] = out[:, half:]


def multiply_back(size, wide, lo_ref, hi_ref, first_ref, second_ref, gf_ref, gs_ref, scratch):
    part = gf_ref.shape[0] // size
    got = jnp.concatenate([lo_ref[...].astype(F32), hi_ref[...].astype(F32)], axis=1)
    grad = blocks(got, size, wide, size, wide).astype(BF16)
    gf_ref[...] = blocks(dot(grad, second_ref[...], 1, 0), wide, part, size, wide).astype(BF16)
    scratch[...] = dot(grad, first_ref[...], 0, 0)
    gs_ref[...] = blocks(reorder(scratch, size, wide), wide, part, size, wide).astype(BF16)


def call(body, outs, *args, scratch=None):
    return pl.pallas_call(
        body,
        out_shape=[jax.ShapeDtypeStruct(s, t) for s, t in outs],
        scratch_shapes=[] if scratch is None else [pltpu.VMEM(scratch, F32)],
        compiler_params=pltpu.CompilerParams(vmem_limit_bytes=48 * 1024 * 1024),
    )(*args)


def exchange(x, axes):
    return lax.all_to_all(x, axes, 0, 0, tiled=True)


def local(pair, grad_out, w_in_out, w_out_out, w_in_in, w_out_in):
    n, _, c = pair.shape
    h = w_out_out.shape[0]
    wide = w_in_out.shape[1]
    size = lax.axis_size(ROW)
    cells = n * n
    half = cells // 2
    part = size // PARTS
    low = (h, cells)
    k_shape = (size * n, part * n)
    pair = pair.reshape(cells, c)
    grad_out = grad_out.reshape(cells, c)

    def apart(first, second, axes):
        got = exchange(jnp.stack([first, second], axis=1), axes)
        return got[:, 0], got[:, 1]

    def product(first, second, group, everyone):
        first, second = apart(first, second, group)
        lo, hi, first, second = call(
            functools.partial(multiply, size, n),
            [((size * size, half), BF16), ((size * size, half), BF16), (k_shape, BF16), (k_shape, BF16)],
            first, second, scratch=k_shape,
        )
        lo, hi = apart(lo, hi, everyone)
        return lo.reshape(PARTS, h, half), hi.reshape(PARTS, h, half), first, second

    def product_back(grad, first, second, group, everyone):
        sent = jnp.broadcast_to(grad.reshape(1, h, 2, half), (PARTS, h, 2, half)).reshape(PARTS * h, 2, half)
        got = exchange(sent, everyone)
        gf, gs = call(
            functools.partial(multiply_back, size, n), [(low, BF16), (low, BF16)],
            got[:, 0], got[:, 1], first, second, scratch=k_shape,
        )
        return apart(gf, gs, group)

    one = (("col_lo",) + ROW, COL + ROW)
    two = (("row_lo",) + COL, ROW + COL)

    left1, right1, proj1, pair_t = call(
        start_one, [(low, BF16), (low, BF16), ((wide, cells), F32), ((c, cells), F32)], pair, w_in_out
    )
    lo, hi, first1, second1 = product(left1, right1, *one)
    left2, right2, proj2, mixed1, mid_t = call(
        middle,
        [(low, BF16), (low, BF16), ((wide, cells), F32), (low, F32), ((c, cells), F32)],
        lo, hi, pair_t, proj1, w_out_out, w_in_in, scratch=(cells, c),
    )
    lo, hi, first2, second2 = product(right2, left2, *two)
    pair_new, grad2, grad_gate2, grad_wout_in = call(
        turn,
        [((n, n, c), F32), (low, BF16), ((c, cells), F32), ((h, c), F32)],
        lo, hi, mid_t, proj2, grad_out, w_out_in, scratch=(cells, c),
    )
    gr2, gl2 = product_back(grad2, first2, second2, *two)
    grad1, grad_gate1, grad_mid, grad_win_in, grad_wout_out = call(
        between,
        [(low, BF16), ((c, cells), F32), ((c, cells), F32), ((wide, c), F32), ((h, c), F32)],
        gl2, gr2, mid_t, proj2, grad_gate2, w_in_in, grad_out, mixed1, proj1, w_out_out, scratch=(cells, c),
    )
    gl1, gr1 = product_back(grad1, first1, second1, *one)
    weight_rows = 2 * (wide + h)
    pair_grad, weights = call(
        last,
        [((cells, c), F32), ((weight_rows, c), BF16)],
        gl1, gr1, pair_t, proj1, grad_gate1, w_in_out, grad_mid, grad_win_in, grad_wout_in, grad_wout_out,
        scratch=(wide, c),
    )

    each = weight_rows // size
    part_sum = jnp.sum(exchange(weights.reshape(size, each, c), ROW).astype(F32), axis=0)
    spread = jnp.broadcast_to(part_sum.astype(BF16)[None], (size, each, c))
    total = jnp.sum(exchange(spread, COL).astype(F32), axis=0) * (1.0 / (n * size))
    spread = jnp.broadcast_to(total.astype(BF16)[None], (size, each, c))
    weights = exchange(spread, ROW).reshape(weight_rows, c).astype(F32)

    def columns(x):
        return jnp.concatenate([x[at : at + c] for at in range(0, wide, c)], axis=1)

    at = wide + h
    return (
        pair_new,
        pair_grad.reshape(n, n, c),
        columns(weights[:wide]),
        weights[wide:at],
        columns(weights[at : at + wide]),
        weights[at + wide :],
    )


def solution(mesh):
    rows, cols = mesh.devices.shape
    fine = Mesh(mesh.devices.reshape(PARTS, rows // PARTS, PARTS, cols // PARTS), ROW + COL)
    cell = P(ROW, COL, None)
    return jax.shard_map(
        local,
        mesh=fine,
        in_specs=(cell, cell, P(), P(), P(), P()),
        out_specs=(cell, cell, P(), P(), P(), P()),
        check_vma=False,
    )
```

time: 1370 us -> 235 us (0.17)
  waiting for transfers between devices: 1250 us -> 0 us
  blocking collectives: 0 us -> 204 us
  matrix products: 39 us -> 0 us
  local copies, waits for them, and re-layouts: 49.6 us -> 18.1 us
  other arithmetic: 18.6 us -> 1.78 us
    psum x2 -> x0, waiting for transfers between devices: 484 us -> none  [local(): lax.psum((grad_win_out, grad_wout_out), ('row', 'col'))]
    reduce_scatter x3 -> x0, waiting for transfers between devices: 328 us -> none  [the longest x1 207 us: local(): lax.psum_scatter(jnp.einsum('ikh,jkh->jih', left_one, piece, preferred_el...]
    all_gather x4 -> x0, waiting for transfers between devices: 248 us -> none  [the longest x1 85.2 us: local(): left_every = lax.all_gather(left_two, 'col', axis=1, tiled=True)]
    all_to_all x0 -> x11, blocking collectives: none -> 204 us  [exchange(): return lax.all_to_all(x, axes, 0, 0, tiled=True)]
    unnamed x11 -> x0, waiting for transfers between devices: 189 us -> none
    dot_general x18 -> x0, matrix products: 39 us -> none  [the longest x1 7.22 us: local(): jnp.einsum('kjh,ijh->ikh', right_two, piece, preferred_element_type=jnp.f...]
    all_gather x4 -> x0, local copies, waits for them, and re-layouts: 21.6 us -> none  [the longest x1 10.7 us: local(): grad_every = lax.all_gather(grad_bf_two, 'row', axis=0, tiled=True)]
    convert_element_type x6 -> x0, local copies, waits for them, and re-layouts: 13.9 us -> none  [the longest x1 4.22 us: local(): jnp.einsum('kih,kjh->ijh', piece, right_two, preferred_element_type=jnp.f...]
  transfers between devices with their start and end apart: 10 -> 0, of which waited for: 10 -> 0; matrix products, arithmetic and copies ran while one was open for 2% -> 0% of each run, Pallas kernels for 0% -> 0%
where the time goes in v1:
time: 235 us; the launch traced here: 234 us
  blocking collectives  204 us (87%)
  local copies, waits for them, and re-layouts  18.1 us (8%)
  Pallas kernels  8.83 us (4%)
    all_to_all x11, blocking collectives, exchange(): return lax.all_to_all(x, axes, 0, 0, tiled=True)  204 us
    unnamed x58, local copies, waits for them, and re-layouts  11.2 us
    pallas_call x9, Pallas kernels, call(): pl.pallas_call(body, out_shape=[jax.ShapeDtypeStruct(s, t) for s, t in ou...  8.83 us

profile of v1, /device:TPU:1, one launch (start us, length us, event | category | flops | bytes accessed | tf_op | source)
XLA Modules:
  0.0 233.9 jit_solution(6801748784560426046)
XLA Ops:
  0.6 0.9 copy-done.2
  1.5 1.0 copy-done.8
  2.5 0.4 shard_map.109
  3.0 0.2 copy.54
  3.2 21.4 %all_to_all.55 = bf16[64,2,576]{2,1,0:T(2,128)(2,1)S(1)} all-to-all(bf16[64,2,576]{2,1,0:T(2,128)(2,1)S(1)} %copy.54), channel_id=1, replica_groups=mesh['row_hi'=4,'row_lo'=4,'col_hi'=4,'col_lo'=4] {'col_lo','row_hi','ro..., dimensions={0} | all-to-all | bytes 294912 | tf_op jit(solution)/shard_map/all_to_all | solution.py:218
  24.6 0.2 fusion.9
  24.8 1.0 shard_map.110
  25.9 0.0 copy-start.13
  25.9 0.1 pad_maximum_fusion
  26.0 0.5 copy-done.11
  26.5 0.0 copy-done.13
  26.6 0.4 copy.57
  27.0 27.9 %all_to_all.56 = bf16[256,2,288]{2,1,0:T(2,128)(2,1)S(1)} all-to-all(bf16[256,2,288]{2,1,0:T(2,128)(2,1)S(1)} %copy.57), channel_id=1, replica_groups=mesh['row_hi'=4,'row_lo'=4,'col_hi'=4,'col_lo'=4] {'col_hi','col_lo','ro..., dimensions={0} | all-to-all | bytes 589824 | tf_op jit(solution)/shard_map/all_to_all | solution.py:218
  54.9 0.5 fusion.5
  55.5 0.0 copy-start.16
  55.5 0.8 copy-done.1
  56.4 0.8 shard_map.111
  57.3 0.6 copy-done.9
  57.9 0.2 copy.60
  58.0 15.8 %all_to_all.57 = bf16[64,2,576]{2,1,0:T(2,128)(2,1)S(1)} all-to-all(bf16[64,2,576]{2,1,0:T(2,128)(2,1)S(1)} %copy.60), channel_id=1, replica_groups=mesh['row_hi'=4,'row_lo'=4,'col_hi'=4,'col_lo'=4] {'row_lo','col_hi','co..., dimensions={0} | all-to-all | bytes 294912 | tf_op jit(solution)/shard_map/all_to_all | solution.py:218
  73.9 0.2 fusion.8
  74.1 1.0 shard_map.112
  75.2 0.1 pad_maximum_fusion.1
  75.2 0.4 copy.63
  75.7 24.5 %all_to_all.58 = bf16[256,2,288]{2,1,0:T(2,128)(2,1)S(1)} all-to-all(bf16[256,2,288]{2,1,0:T(2,128)(2,1)S(1)} %copy.63), channel_id=1, replica_groups=mesh['row_hi'=4,'row_lo'=4,'col_hi'=4,'col_lo'=4] {'row_hi','row_lo','co..., dimensions={0} | all-to-all | bytes 589824 | tf_op jit(solution)/shard_map/all_to_all | solution.py:218
  100.2 0.5 fusion.4
  100.8 0.0 copy-start
  100.8 0.9 copy-done
  101.7 1.1 shard_map.113
  102.9 0.7 copy-done.6
  103.6 0.6 copy-done.17
  104.2 0.1 broadcast_in_dim.12
  104.3 0.2 broadcast_in_dim.13
  104.6 24.0 %all_to_all.59 = bf16[256,2,288]{2,1,0:T(2,128)(2,1)S(1)} all-to-all(bf16[256,2,288]{2,1,0:T(2,128)(2,1)S(1)} %bitcast.89), channel_id=1, replica_groups=mesh['row_hi'=4,'row_lo'=4,'col_hi'=4,'col_lo'=4] {'row_hi','row_lo','co..., dimensions={0} | all-to-all | bytes 589824 | tf_op jit(solution)/shard_map/all_to_all | solution.py:218
  128.6 0.5 fusion.3
  129.2 1.0 shard_map.114
  130.2 0.2 copy.68
  130.4 15.8 %all_to_all.60 = bf16[64,2,576]{2,1,0:T(2,128)(2,1)S(1)} all-to-all(bf16[64,2,576]{2,1,0:T(2,128)(2,1)S(1)} %copy.68), channel_id=1, replica_groups=mesh['row_hi'=4,'row_lo'=4,'col_hi'=4,'col_lo'=4] {'row_lo','col_hi','co..., dimensions={0} | all-to-all | bytes 294912 | tf_op jit(solution)/shard_map/all_to_all | solution.py:218
  146.2 0.2 fusion.7
  146.5 0.9 copy-done.7
  147.4 0.0 copy-done.10
  147.5 1.1 shard_map.115
  148.5 0.7 copy-done.4
  149.2 0.6 copy-done.15
  149.9 0.6 copy-done.19
  150.5 1.0 broadcast_in_dim.28
  151.5 0.2 broadcast_in_dim.29
  151.7 23.6 %all_to_all.61 = bf16[256,2,288]{2,1,0:T(2,128)(2,1)S(1)} all-to-all(bf16[256,2,288]{2,1,0:T(2,128)(2,1)S(1)} %bitcast.90), channel_id=1, replica_groups=mesh['row_hi'=4,'row_lo'=4,'col_hi'=4,'col_lo'=4] {'col_hi','col_lo','ro..., dimensions={0} | all-to-all | bytes 589824 | tf_op jit(solution)/shard_map/all_to_all | solution.py:218
  175.4 0.5 fusion.2
  176.0 0.8 copy-done.12
  176.8 0.0 copy-done.14
  176.9 1.0 shard_map.116
  177.9 0.2 copy.73
  178.1 14.4 %all_to_all.62 = bf16[64,2,576]{2,1,0:T(2,128)(2,1)S(1)} all-to-all(bf16[64,2,576]{2,1,0:T(2,128)(2,1)S(1)} %copy.73), channel_id=1, replica_groups=mesh['row_hi'=4,'row_lo'=4,'col_hi'=4,'col_lo'=4] {'col_lo','row_hi','ro..., dimensions={0} | all-to-all | bytes 294912 | tf_op jit(solution)/shard_map/all_to_all | solution.py:218
  192.4 0.2 fusion.6
  192.8 0.9 copy-done.5
  193.6 0.0 copy-done.3
  193.7 1.4 shard_map.117
  195.1 9.8 %all_to_all.63 = bf16[16,56,128]{2,1,0:T(8,128)(2,1)S(1)} all-to-all(bf16[16,56,128]{2,1,0:T(8,128)(2,1)S(1)} %bitcast.76), channel_id=1, replica_groups=mesh['row_hi'=4,'row_lo'=4,'col_hi'=4,'col_lo'=4] {'row_hi','row_lo'}, dimensions={0} | all-to-all | bytes 458752 | tf_op jit(solution)/shard_map/all_to_all | solution.py:218
  204.9 14.4 %all_to_all.64 = bf16[16,56,128]{2,1,0:T(8,128)(2,1)S(1)} all-to-all(bf16[16,56,128]{2,1,0:T(8,128)(2,1)S(1)} %broadcast_in_dim.30), channel_id=1, replica_groups=mesh['row_hi'=4,'row_lo'=4,'col_hi'=4,'col_lo'=4] {'col_hi','col_lo'}, dimensions={0} | all-to-all | bytes 458752 | tf_op jit(solution)/shard_map/all_to_all | solution.py:218
  219.5 12.3 %all_to_all.65 = bf16[16,56,128]{2,1,0:T(8,128)(2,1)S(1)} all-to-all(bf16[16,56,128]{2,1,0:T(8,128)(2,1)S(1)} %broadcast_in_dim.31), channel_id=1, replica_groups=mesh['row_hi'=4,'row_lo'=4,'col_hi'=4,'col_lo'=4] {'row_hi','row_lo'}, dimensions={0} | all-to-all | bytes 458752 | tf_op jit(solution)/shard_map/all_to_all | solution.py:218
  231.8 0.6 fusion
  232.5 0.7 pad_maximum_fusion.3
  233.2 0.7 pad_maximum_fusion.2
  (49 shorter events, 0.7 us)
Async XLA Ops:
  0.6 0.9 copy-start.2
  1.5 1.0 copy-start.8
  25.9 0.6 copy-start.11
  25.9 0.7 copy-start.13
  55.5 0.9 copy-start.1
  55.5 0.9 copy-start.16
  57.2 0.7 copy-start.9
  100.8 1.0 copy-start
  100.8 1.0 copy-start.21
  102.9 0.7 copy-start.6
  103.6 0.6 copy-start.17
  146.4 1.0 copy-start.7
  146.5 1.0 copy-start.10
  148.5 0.7 copy-start.4
  149.2 0.6 copy-start.15
  149.9 0.6 copy-start.19
  175.9 0.9 copy-start.12
  176.0 0.9 copy-start.14
  192.7 1.0 copy-start.5
  192.7 1.0 copy-start.3
  192.7 1.0 copy-start.18
  192.7 0.9 copy-start.20

commit v2 on v1

v2 whole, which is shorter than its diff:
```python
import functools

import jax
import jax.numpy as jnp
import numpy as np
from jax import lax
from jax.experimental import pallas as pl
from jax.experimental.pallas import tpu as pltpu
from jax.sharding import Mesh
from jax.sharding import PartitionSpec as P

EPS = 1e-05
F32 = jnp.float32
BF16 = jnp.bfloat16
PARTS = 4
ROW = ("row_hi", "row_lo")
COL = ("col_y", "col_hi", "col_lo")
NEAR = ROW + ("col_y",)
FAR = ("col_hi", "col_lo")


def dot(a, b, ca, cb):
    return lax.dot_general(a, b, (((ca,), (cb,)), ((), ())), preferred_element_type=F32)


def norm(x):
    center = x - jnp.mean(x, axis=0, keepdims=True)
    rstd = lax.rsqrt(jnp.mean(center * center, axis=0, keepdims=True) + EPS)
    return center * rstd, rstd


def norm_back(grad, normed, rstd):
    return rstd * (
        grad
        - jnp.mean(grad, axis=0, keepdims=True)
        - normed * jnp.mean(grad * normed, axis=0, keepdims=True)
    )


def swap_cells(ref, n):
    return jnp.concatenate([ref[pl.ds(j, n, stride=n), :] for j in range(n)], axis=0)


def project(x, w_in, proj_ref, sent_ref, order):
    h = sent_ref.shape[0]
    normed, _ = norm(x)
    proj = dot(w_in, normed.astype(BF16), 0, 0)
    proj_ref[...] = proj
    for at, place in zip((0, 2 * h), order):
        gated = jax.nn.sigmoid(proj[at + h : at + 2 * h]) * proj[at : at + h]
        sent_ref[:, place, :] = gated.astype(BF16)


def project_back(x, proj_ref, w_in, gl, gr, grad_gate, grad_w_ref):
    h = gl.shape[0]
    normed, rstd = norm(x)
    sa = jax.nn.sigmoid(proj_ref[h : 2 * h, :])
    sb = jax.nn.sigmoid(proj_ref[3 * h : 4 * h, :])
    gate = jax.nn.sigmoid(proj_ref[4 * h :, :])
    gla, grb = gl * sa, gr * sb
    grad = jnp.concatenate(
        [
            gla,
            gla * proj_ref[:h, :] * (1 - sa),
            grb,
            grb * proj_ref[2 * h : 3 * h, :] * (1 - sb),
            grad_gate * gate * (1 - gate),
        ],
        axis=0,
    ).astype(BF16)
    low = normed.astype(BF16)
    c = x.shape[0]
    for at in range(0, grad.shape[0], c):
        grad_w_ref[at : at + c, :] = dot(low, grad[at : at + c], 1, 1)
    return norm_back(dot(w_in, grad, 1, 0), normed, rstd)


def finish(mixed, w_out):
    normed, rstd = norm(mixed)
    post = normed.astype(BF16)
    return dot(w_out, post, 0, 0), normed, rstd, post


def finish_back(grad_new, gate, out, normed, rstd, post, w_out):
    grad_gate = grad_new * out
    grad_proj = (grad_new * gate).astype(BF16)
    grad_w = dot(post, grad_proj, 1, 1)
    return norm_back(dot(w_out, grad_proj, 1, 0), normed, rstd), grad_gate, grad_w


def summed(got_ref):
    h = got_ref.shape[0] // PARTS

    def total(k):
        parts = [got_ref[q * h : (q + 1) * h, k, :].astype(F32) for q in range(PARTS)]
        return (parts[0] + parts[1]) + (parts[2] + parts[3])

    return jnp.concatenate([total(0), total(1)], axis=1)


def send_halves(x, sent_ref):
    half = sent_ref.shape[2]
    for at in range(0, sent_ref.shape[0], x.shape[0]):
        sent_ref[at : at + x.shape[0], 0, :] = x[:, :half]
        sent_ref[at : at + x.shape[0], 1, :] = x[:, half:]


def start_one(pair_ref, w_ref, sent_ref, proj_ref, pair_t_ref):
    x = pair_ref[...].T
    pair_t_ref[...] = x
    project(x, w_ref[...], proj_ref, sent_ref, (0, 1))


def middle(
    got_ref, pair_t_ref, proj1_ref, w_out_ref, w_in_ref,
    sent_ref, proj2_ref, mixed_ref, mid_ref, scratch,
):
    h = sent_ref.shape[0]
    mixed = summed(got_ref)
    mixed_ref[...] = mixed
    out, *_ = finish(mixed, w_out_ref[...])
    mid = pair_t_ref[...] + jax.nn.sigmoid(proj1_ref[4 * h :, :]) * out
    scratch[...] = mid.T
    mid = swap_cells(scratch, int(round(scratch.shape[0] ** 0.5))).T
    mid_ref[...] = mid
    project(mid, w_in_ref[...], proj2_ref, sent_ref, (1, 0))


def turn(
    got_ref, mid_ref, proj_ref, grad_out_ref, w_out_ref,
    new_ref, sent_ref, grad_gate_ref, grad_w_ref, scratch,
):
    h = got_ref.shape[0] // PARTS
    n = new_ref.shape[0]
    out, normed, rstd, post = finish(summed(got_ref), w_out_ref[...])
    gate = jax.nn.sigmoid(proj_ref[4 * h :, :])
    new = (mid_ref[...] + gate * out).T
    scratch[...] = new
    new_ref[...] = swap_cells(scratch, n).reshape(new_ref.shape)
    grad_new = swap_cells(grad_out_ref, n).T
    grad, grad_gate, grad_w = finish_back(grad_new, gate, out, normed, rstd, post, w_out_ref[...])
    send_halves(grad.astype(BF16), sent_ref)
    grad_gate_ref[...] = grad_gate
    grad_w_ref[...] = grad_w


def between(
    got_ref, mid_ref, proj2_ref, grad_gate2_ref, w_in_ref, grad_out_ref, mixed_ref, proj1_ref, w_out_ref,
    sent_ref, grad_gate_ref, grad_mid_ref, grad_win_ref, grad_wout_ref, scratch,
):
    h = got_ref.shape[0]
    low = project_back(
        mid_ref[...], proj2_ref, w_in_ref[...], got_ref[:, 1, :].astype(F32), got_ref[:, 0, :].astype(F32),
        grad_gate2_ref[...], grad_win_ref,
    )
    scratch[...] = low.T
    n = int(round(scratch.shape[0] ** 0.5))
    grad_mid = (grad_out_ref[...] + swap_cells(scratch, n)).T
    grad_mid_ref[...] = grad_mid
    w_out = w_out_ref[...]
    out, normed, rstd, post = finish(mixed_ref[...], w_out)
    gate = jax.nn.sigmoid(proj1_ref[4 * h :, :])
    grad, grad_gate, grad_w = finish_back(grad_mid, gate, out, normed, rstd, post, w_out)
    send_halves(grad.astype(BF16), sent_ref)
    grad_gate_ref[...] = grad_gate
    grad_wout_ref[...] = grad_w


def last(
    got_ref, pair_t_ref, proj_ref, grad_gate_ref, w_in_ref, grad_mid_ref, win2_ref, wout2_ref, wout1_ref,
    pair_grad_ref, weights_ref, scratch,
):
    low = project_back(
        pair_t_ref[...], proj_ref, w_in_ref[...], got_ref[:, 0, :].astype(F32), got_ref[:, 1, :].astype(F32),
        grad_gate_ref[...], scratch,
    )
    pair_grad_ref[...] = (grad_mid_ref[...] + low).T
    weights_ref[...] = jnp.concatenate(
        [scratch[...], wout1_ref[...], win2_ref[...], wout2_ref[...]], axis=0
    ).astype(BF16)


def blocks(x, outer, inner, size, wide):
    rows = []
    for r in range(inner):
        rows.append(
            jnp.concatenate(
                [x[o * size : (o + 1) * size, r * wide : (r + 1) * wide] for o in range(outer)], axis=1
            )
        )
    return jnp.concatenate(rows, axis=0)


def reorder(ref, outer, inner):
    return jnp.concatenate([ref[pl.ds(r, outer, stride=inner), :] for r in range(inner)], axis=0)


def multiply(size, wide, got_ref, sent_ref, first_out_ref, second_out_ref, scratch):
    part = got_ref.shape[0] // size
    first = blocks(got_ref[:, 0, :].astype(F32), part, wide, size, wide).astype(BF16)
    scratch[...] = blocks(got_ref[:, 1, :].astype(F32), part, wide, size, wide)
    second = reorder(scratch, wide, size).astype(BF16)
    first_out_ref[...] = first
    second_out_ref[...] = second
    out = blocks(dot(first, second, 1, 1), wide, size, size, wide).astype(BF16)
    send_halves(out, sent_ref)


def multiply_back(size, wide, got_ref, first_ref, second_ref, sent_ref, scratch):
    part = sent_ref.shape[0] // size
    got = jnp.concatenate([got_ref[:, 0, :].astype(F32), got_ref[:, 1, :].astype(F32)], axis=1)
    grad = blocks(got, size, wide, size, wide).astype(BF16)
    sent_ref[:, 0, :] = blocks(dot(grad, second_ref[...], 1, 0), wide, part, size, wide).astype(BF16)
    scratch[...] = dot(grad, first_ref[...], 0, 0)
    sent_ref[:, 1, :] = blocks(reorder(scratch, size, wide), wide, part, size, wide).astype(BF16)


def sum_and_spread(got_ref, sent_ref):
    total = got_ref[0].astype(F32)
    for i in range(1, got_ref.shape[0]):
        total += got_ref[i].astype(F32)
    total = total.astype(BF16)
    for i in range(sent_ref.shape[0]):
        sent_ref[i] = total


def unpack(scale, got_ref, *out_refs):
    at = 0
    for ref in out_refs:
        c = got_ref.shape[1]
        rows = ref.shape[0]
        for lane in range(0, ref.shape[1], c):
            ref[:, lane : lane + c] = got_ref[at : at + rows, :].astype(F32) * scale
            at += rows


def call(body, outs, *args, scratch=None):
    return pl.pallas_call(
        body,
        out_shape=[jax.ShapeDtypeStruct(s, t) for s, t in outs],
        scratch_shapes=[] if scratch is None else [pltpu.VMEM(scratch, F32)],
        compiler_params=pltpu.CompilerParams(vmem_limit_bytes=16 * 1024 * 1024),
    )(*args)


def exchange(x, axes):
    return lax.all_to_all(x, axes, 0, 0, tiled=True)


def local(pair, grad_out, w_in_out, w_out_out, w_in_in, w_out_in):
    n, _, c = pair.shape
    h = w_out_out.shape[0]
    wide = w_in_out.shape[1]
    size = lax.axis_size(ROW)
    cells = n * n
    part = size // PARTS
    low = (h, cells)
    k_shape = (size * n, part * n)
    pair = pair.reshape(cells, c)
    grad_out = grad_out.reshape(cells, c)

    cell_array = ((c, cells), F32)
    near = ((h, 2, cells), BF16)
    all_devices = ((size * size, 2, cells // 2), BF16)

    def product(sent, group, everyone):
        sent, first, second = call(
            functools.partial(multiply, size, n),
            [all_devices, (k_shape, BF16), (k_shape, BF16)],
            exchange(sent, group), scratch=k_shape,
        )
        return exchange(sent, everyone), first, second

    def product_back(sent, first, second, group, everyone):
        sent, = call(
            functools.partial(multiply_back, size, n), [near], exchange(sent, everyone), first, second, scratch=k_shape
        )
        return exchange(sent, group)

    one = (("col_lo",) + ROW, COL + ROW)
    two = (("row_lo",) + COL, ROW + COL)

    sent, proj1, pair_t = call(start_one, [near, ((wide, cells), F32), cell_array], pair, w_in_out)
    got, first1, second1 = product(sent, *one)
    sent, proj2, mixed1, mid_t = call(
        middle,
        [near, ((wide, cells), F32), (low, F32), cell_array],
        got, pair_t, proj1, w_out_out, w_in_in, scratch=(cells, c),
    )
    got, first2, second2 = product(sent, *two)
    pair_new, sent, grad_gate2, grad_wout_in = call(
        turn,
        [((n, n, c), F32), all_devices, cell_array, ((h, c), F32)],
        got, mid_t, proj2, grad_out, w_out_in, scratch=(cells, c),
    )
    got = product_back(sent, first2, second2, *two)
    sent, grad_gate1, grad_mid, grad_win_in, grad_wout_out = call(
        between,
        [all_devices, cell_array, cell_array, ((wide, c), F32), ((h, c), F32)],
        got, mid_t, proj2, grad_gate2, w_in_in, grad_out, mixed1, proj1, w_out_out, scratch=(cells, c),
    )
    got = product_back(sent, first1, second1, *one)
    weight_rows = 2 * (wide + h)
    pair_grad, weights = call(
        last,
        [((cells, c), F32), ((weight_rows, c), BF16)],
        got, pair_t, proj1, grad_gate1, w_in_out, grad_mid, grad_win_in, grad_wout_in, grad_wout_out,
        scratch=(wide, c),
    )

    near_count, far_count = lax.axis_size(NEAR), lax.axis_size(FAR)
    each = weight_rows // near_count
    got = exchange(weights.reshape(near_count, each, c), NEAR)
    sent, = call(sum_and_spread, [((far_count, each, c), BF16)], got)
    sent, = call(sum_and_spread, [((near_count, each, c), BF16)], exchange(sent, FAR))
    outs = call(
        functools.partial(unpack, 1.0 / (n * size)),
        [((c, wide), F32), ((h, c), F32), ((c, wide), F32), ((h, c), F32)],
        exchange(sent, NEAR).reshape(weight_rows, c),
    )
    return (pair_new, pair_grad.reshape(n, n, c), *outs)


def solution(mesh):
    rows, cols = mesh.devices.shape
    fine = Mesh(mesh.devices.reshape(PARTS, rows // PARTS, 2, PARTS // 2, cols // PARTS), ROW + COL)
    cell = P(ROW, COL, None)
    return jax.shard_map(
        local,
        mesh=fine,
        in_specs=(cell, cell, P(), P(), P(), P()),
        out_specs=(cell, cell, P(), P(), P(), P()),
        check_vma=False,
    )
```

time: 235 us -> 221 us (0.940)
  local copies, waits for them, and re-layouts: 18.1 us -> 1.97 us
  Pallas kernels: 8.83 us -> 12.1 us
    unnamed x58 -> x14, local copies, waits for them, and re-layouts: 11.2 us -> 1.88 us
    slice x10 -> x0, local copies, waits for them, and re-layouts: 3.76 us -> none  [the longest x6 2.01 us: apart(): return (got[:, 0], got[:, 1])]
    pallas_call x9 -> x12, Pallas kernels: 8.83 us -> 12.1 us  [call(): pl.pallas_call(body, out_shape=[jax.ShapeDtypeStruct(s, t) for s, t in ou...]
where the time goes in v2:
time: 221 us; the launch traced here: 220 us
  blocking collectives  205 us (93%)
  Pallas kernels  12.1 us (5%)
    all_to_all x11, blocking collectives, exchange(): return lax.all_to_all(x, axes, 0, 0, tiled=True)  205 us
    pallas_call x12, Pallas kernels, call(): pl.pallas_call(body, out_shape=[jax.ShapeDtypeStruct(s, t) for s, t in ou...  12.1 us

profile of v2, /device:TPU:1, one launch (start us, length us, event | category | flops | bytes accessed | tf_op | source)
XLA Modules:
  0.0 220.0 jit_solution(15146985195316693721)
XLA Ops:
  0.6 0.0 copy-start.2
  0.6 0.9 copy-done.2
  1.5 0.0 copy-start.4
  1.5 1.0 copy-done.4
  2.5 0.5 shard_map.109
  3.0 21.4 %all_to_all.55.got_ref = bf16[64,2,576]{2,1,0:T(2,128)(2,1)S(1)} all-to-all(bf16[64,2,576]{2,1,0:T(2,128)(2,1)S(1)} %get-tuple-element.34), channel_id=1, replica_groups=mesh['row_hi'=4,'row_lo'=4,'col_y'=2,'col_hi'=2,'col_lo'=4] {'col_lo','r..., dimensions={0} | all-to-all | bytes 294912 | tf_op jit(solution)/shard_map/all_to_all | solution.py:247
  24.4 1.6 shard_map.110
  26.0 0.0 copy-start.1
  26.0 0.0 copy-start.5
  26.0 27.9 %all_to_all.56.got_ref = bf16[256,2,288]{2,1,0:T(2,128)(2,1)S(1)} all-to-all(bf16[256,2,288]{2,1,0:T(2,128)(2,1)S(1)} %get-tuple-element.35), channel_id=1, replica_groups=mesh['row_hi'=4,'row_lo'=4,'col_y'=2,'col_hi'=2,'col_lo'=4] {'col_y','co..., dimensions={0} | all-to-all | bytes 589824 | tf_op jit(solution)/shard_map/all_to_all | solution.py:247
  53.9 0.0 copy-done.1
  53.9 0.0 copy-done.5
  54.0 1.0 shard_map.111
  54.9 15.8 %all_to_all.57.got_ref = bf16[64,2,576]{2,1,0:T(2,128)(2,1)S(1)} all-to-all(bf16[64,2,576]{2,1,0:T(2,128)(2,1)S(1)} %get-tuple-element.38), channel_id=1, replica_groups=mesh['row_hi'=4,'row_lo'=4,'col_y'=2,'col_hi'=2,'col_lo'=4] {'row_lo','c..., dimensions={0} | all-to-all | bytes 294912 | tf_op jit(solution)/shard_map/all_to_all | solution.py:247
  70.7 1.6 shard_map.112
  72.3 0.0 copy-start
  72.3 0.0 copy-start.6
  72.3 24.5 %all_to_all.58.got_ref = bf16[256,2,288]{2,1,0:T(2,128)(2,1)S(1)} all-to-all(bf16[256,2,288]{2,1,0:T(2,128)(2,1)S(1)} %get-tuple-element.39), channel_id=1, replica_groups=mesh['row_hi'=4,'row_lo'=4,'col_y'=2,'col_hi'=2,'col_lo'=4] {'row_hi','r..., dimensions={0} | all-to-all | bytes 589824 | tf_op jit(solution)/shard_map/all_to_all | solution.py:247
  96.9 0.0 copy-done
  96.9 0.0 copy-done.6
  96.9 1.2 shard_map.113
  98.1 23.8 %all_to_all.59.got_ref = bf16[256,2,288]{2,1,0:T(2,128)(2,1)S(1)} all-to-all(bf16[256,2,288]{2,1,0:T(2,128)(2,1)S(1)} %get-tuple-element.43), channel_id=1, replica_groups=mesh['row_hi'=4,'row_lo'=4,'col_y'=2,'col_hi'=2,'col_lo'=4] {'row_hi','r..., dimensions={0} | all-to-all | bytes 589824 | tf_op jit(solution)/shard_map/all_to_all | solution.py:247
  121.9 1.2 shard_map.114
  123.2 15.8 %all_to_all.60.got_ref = bf16[64,2,576]{2,1,0:T(2,128)(2,1)S(1)} all-to-all(bf16[64,2,576]{2,1,0:T(2,128)(2,1)S(1)} %shard_map.114), channel_id=1, replica_groups=mesh['row_hi'=4,'row_lo'=4,'col_y'=2,'col_hi'=2,'col_lo'=4] {'row_lo','c..., dimensions={0} | all-to-all | bytes 294912 | tf_op jit(solution)/shard_map/all_to_all | solution.py:247
  139.0 1.4 shard_map.115
  140.4 23.6 %all_to_all.61.got_ref = bf16[256,2,288]{2,1,0:T(2,128)(2,1)S(1)} all-to-all(bf16[256,2,288]{2,1,0:T(2,128)(2,1)S(1)} %get-tuple-element.48), channel_id=1, replica_groups=mesh['row_hi'=4,'row_lo'=4,'col_y'=2,'col_hi'=2,'col_lo'=4] {'col_y','co..., dimensions={0} | all-to-all | bytes 589824 | tf_op jit(solution)/shard_map/all_to_all | solution.py:247
  164.0 1.2 shard_map.116
  165.2 0.0 copy-start.3
  165.2 14.5 %all_to_all.62.got_ref = bf16[64,2,576]{2,1,0:T(2,128)(2,1)S(1)} all-to-all(bf16[64,2,576]{2,1,0:T(2,128)(2,1)S(1)} %shard_map.116), channel_id=1, replica_groups=mesh['row_hi'=4,'row_lo'=4,'col_y'=2,'col_hi'=2,'col_lo'=4] {'col_lo','r..., dimensions={0} | all-to-all | bytes 294912 | tf_op jit(solution)/shard_map/all_to_all | solution.py:247
  179.7 0.0 copy-done.3
  179.7 1.5 shard_map.117
  181.3 12.9 %all_to_all.63.got_ref = bf16[32,28,128]{2,1,0:T(8,128)(2,1)S(1)} all-to-all(bf16[32,28,128]{2,1,0:T(8,128)(2,1)S(1)} %reshape.30), channel_id=1, replica_groups=mesh['row_hi'=4,'row_lo'=4,'col_y'=2,'col_hi'=2,'col_lo'=4] {'row_hi','r..., dimensions={0} | all-to-all | bytes 458752 | tf_op jit(solution)/shard_map/all_to_all | solution.py:247
  194.2 0.1 shard_map.118
  194.3 11.1 %all_to_all.64.got_ref = bf16[8,28,128]{2,1,0:T(8,128)(2,1)S(1)} all-to-all(bf16[8,28,128]{2,1,0:T(8,128)(2,1)S(1)} %shard_map.118), channel_id=1, replica_groups=mesh['row_hi'=4,'row_lo'=4,'col_y'=2,'col_hi'=2,'col_lo'=4] {'col_hi','c..., dimensions={0} | all-to-all | bytes 114688 | tf_op jit(solution)/shard_map/all_to_all | solution.py:247
  205.4 13.7 %all_to_all.65 = bf16[32,28,128]{2,1,0:T(8,128)(2,1)S(1)} all-to-all(bf16[32,28,128]{2,1,0:T(8,128)(2,1)S(1)} %shard_map.119), channel_id=1, replica_groups=mesh['row_hi'=4,'row_lo'=4,'col_y'=2,'col_hi'=2,'col_lo'=4] {'row_hi','r..., dimensions={0} | all-to-all | bytes 458752 | tf_op jit(solution)/shard_map/all_to_all | solution.py:247
  219.2 0.8 shard_map.120
  (3 shorter events, 0.1 us)
Async XLA Ops:
  0.6 0.9 copy-start.2
  1.5 1.0 copy-start.4
  26.0 27.9 %copy-start.1 = (bf16[128,384]{1,0:T(8,128)(2,1)S(1)}, bf16[128,384]{1,0:T(8,128)(2,1)}, u32[]{:S(2)}) copy-start(bf16[128,384]{1,0:T(8,128)(2,1)} %w_in_ref.4) | copy-start | bytes 294916
  26.0 27.9 %copy-start.5 = (bf16[64,128]{1,0:T(8,128)(2,1)S(1)}, bf16[64,128]{1,0:T(8,128)(2,1)}, u32[]{:S(2)}) copy-start(bf16[64,128]{1,0:T(8,128)(2,1)} %w_out_ref.5) | copy-start | bytes 49156
  72.3 24.6 %copy-start = (f32[24,24,128]{2,1,0:T(8,128)S(1)}, f32[24,24,128]{2,1,0:T(8,128)}, u32[]{:S(2)}) copy-start(f32[24,24,128]{2,1,0:T(8,128)} %param.7) | copy-start | bytes 884740
  72.3 24.5 %copy-start.6 = (bf16[64,128]{1,0:T(8,128)(2,1)S(1)}, bf16[64,128]{1,0:T(8,128)(2,1)}, u32[]{:S(2)}) copy-start(bf16[64,128]{1,0:T(8,128)(2,1)} %w_out_ref.4) | copy-start | bytes 49156
  165.2 14.5 %copy-start.3 = (bf16[128,384]{1,0:T(8,128)(2,1)S(1)}, bf16[128,384]{1,0:T(8,128)(2,1)}, u32[]{:S(2)}) copy-start(bf16[128,384]{1,0:T(8,128)(2,1)} %w_in_ref.5) | copy-start | bytes 294916

commit v3 on v2

--- a/solution.py
+++ b/solution.py
@@ -2,7 +2,6 @@
 
 import jax
 import jax.numpy as jnp
-import numpy as np
 from jax import lax
 from jax.experimental import pallas as pl
 from jax.experimental.pallas import tpu as pltpu
@@ -13,10 +12,11 @@
 F32 = jnp.float32
 BF16 = jnp.bfloat16
 PARTS = 4
-ROW = ("row_hi", "row_lo")
-COL = ("col_y", "col_hi", "col_lo")
-NEAR = ROW + ("col_y",)
-FAR = ("col_hi", "col_lo")
+SPLIT = 2
+ROW = ("row_a", "row_q", "row_b")
+COL = ("col_a", "col_q", "col_b")
+NEAR = ("col_a",) + ROW
+FAR = ("col_q", "col_b")
 
 
 def dot(a, b, ca, cb):
@@ -51,7 +51,7 @@
         sent_ref[:, place, :] = gated.astype(BF16)
 
 
-def project_back(x, proj_ref, w_in, gl, gr, grad_gate, grad_w_ref):
+def project_back(x, proj_ref, w_in, gl, gr, grad_gate):
     h = gl.shape[0]
     normed, rstd = norm(x)
     sa = jax.nn.sigmoid(proj_ref[h : 2 * h, :])
@@ -68,11 +68,7 @@
         ],
         axis=0,
     ).astype(BF16)
-    low = normed.astype(BF16)
-    c = x.shape[0]
-    for at in range(0, grad.shape[0], c):
-        grad_w_ref[at : at + c, :] = dot(low, grad[at : at + c], 1, 1)
-    return norm_back(dot(w_in, grad, 1, 0), normed, rstd)
+    return norm_back(dot(w_in, grad, 1, 0), normed, rstd), normed.astype(BF16), grad
 
 
 def finish(mixed, w_out):
@@ -88,21 +84,23 @@
     return norm_back(dot(w_out, grad_proj, 1, 0), normed, rstd), grad_gate, grad_w
 
 
+def owners(count, h):
+    run = h // SPLIT
+    return [(at, (at // run // PARTS) * run, run) for at in range(0, count, run)]
+
+
 def summed(got_ref):
-    h = got_ref.shape[0] // PARTS
+    count = got_ref.shape[0]
+    h = count // PARTS
 
     def total(k):
-        parts = [got_ref[q * h : (q + 1) * h, k, :].astype(F32) for q in range(PARTS)]
-        return (parts[0] + parts[1]) + (parts[2] + parts[3])
+        sums = {}
+        for at, channel, run in owners(count, h):
+            part = got_ref[at : at + run, k, :].astype(F32)
+            sums[channel] = sums[channel] + part if channel in sums else part
+        return jnp.concatenate(list(sums.values()), axis=0)
 
     return jnp.concatenate([total(0), total(1)], axis=1)
-
-
-def send_halves(x, sent_ref):
-    half = sent_ref.shape[2]
-    for at in range(0, sent_ref.shape[0], x.shape[0]):
-        sent_ref[at : at + x.shape[0], 0, :] = x[:, :half]
-        sent_ref[at : at + x.shape[0], 1, :] = x[:, half:]
 
 
 def start_one(pair_ref, w_ref, sent_ref, proj_ref, pair_t_ref):
@@ -139,21 +137,25 @@
     new_ref[...] = swap_cells(scratch, n).reshape(new_ref.shape)
     grad_new = swap_cells(grad_out_ref, n).T
     grad, grad_gate, grad_w = finish_back(grad_new, gate, out, normed, rstd, post, w_out_ref[...])
-    send_halves(grad.astype(BF16), sent_ref)
+    grad = grad.astype(BF16)
+    half = sent_ref.shape[2]
+    for at, channel, run in owners(sent_ref.shape[0], h):
+        for k in range(2):
+            sent_ref[at : at + run, k, :] = grad[channel : channel + run, k * half : (k + 1) * half]
     grad_gate_ref[...] = grad_gate
     grad_w_ref[...] = grad_w
 
 
 def between(
     got_ref, mid_ref, proj2_ref, grad_gate2_ref, w_in_ref, grad_out_ref, mixed_ref, proj1_ref, w_out_ref,
-    sent_ref, grad_gate_ref, grad_mid_ref, grad_win_ref, grad_wout_ref, scratch,
+    sent_ref, grad_gate_ref, grad_mid_ref, grad_wout_ref, scratch,
 ):
-    h = got_ref.shape[0]
-    low = project_back(
+    h, _, cells = got_ref.shape
+    back, low, grad_proj = project_back(
         mid_ref[...], proj2_ref, w_in_ref[...], got_ref[:, 1, :].astype(F32), got_ref[:, 0, :].astype(F32),
-        grad_gate2_ref[...], grad_win_ref,
-    )
-    scratch[...] = low.T
+        grad_gate2_ref[...],
+    )
+    scratch[...] = back.T
     n = int(round(scratch.shape[0] ** 0.5))
     grad_mid = (grad_out_ref[...] + swap_cells(scratch, n)).T
     grad_mid_ref[...] = grad_mid
@@ -161,23 +163,37 @@
     out, normed, rstd, post = finish(mixed_ref[...], w_out)
     gate = jax.nn.sigmoid(proj1_ref[4 * h :, :])
     grad, grad_gate, grad_w = finish_back(grad_mid, gate, out, normed, rstd, post, w_out)
-    send_halves(grad.astype(BF16), sent_ref)
     grad_gate_ref[...] = grad_gate
     grad_wout_ref[...] = grad_w
+    grad = grad.astype(BF16)
+    half = cells // 2
+    count = sent_ref.shape[0]
+    wide = sent_ref.shape[2] - half
+    pairs = low.shape[0] // 2
+    weights = [
+        dot(low, grad_proj[at : at + wide], 1, 1).astype(BF16) for at in range(0, grad_proj.shape[0], wide)
+    ]
+    for at, channel, run in owners(count, h):
+        block, first = at // pairs, at % pairs
+        for k in range(2):
+            rows = weights[block][k * pairs + first : k * pairs + first + run]
+            sent_ref[at : at + run, k, :] = jnp.concatenate(
+                [grad[channel : channel + run, k * half : (k + 1) * half], rows], axis=1
+            )
 
 
 def last(
-    got_ref, pair_t_ref, proj_ref, grad_gate_ref, w_in_ref, grad_mid_ref, win2_ref, wout2_ref, wout1_ref,
-    pair_grad_ref, weights_ref, scratch,
+    got_ref, pair_t_ref, proj_ref, grad_gate_ref, w_in_ref, grad_mid_ref, wout1_ref, wout2_ref,
+    pair_grad_ref, weights_ref,
 ):
-    low = project_back(
+    back, low, grad_proj = project_back(
         pair_t_ref[...], proj_ref, w_in_ref[...], got_ref[:, 0, :].astype(F32), got_ref[:, 1, :].astype(F32),
-        grad_gate_ref[...], scratch,
-    )
-    pair_grad_ref[...] = (grad_mid_ref[...] + low).T
-    weights_ref[...] = jnp.concatenate(
-        [scratch[...], wout1_ref[...], win2_ref[...], wout2_ref[...]], axis=0
-    ).astype(BF16)
+        grad_gate_ref[...],
+    )
+    c = low.shape[0]
+    rows = [dot(low, grad_proj[at : at + c], 1, 1) for at in range(0, grad_proj.shape[0], c)]
+    weights_ref[...] = jnp.concatenate(rows + [wout1_ref[...], wout2_ref[...]], axis=0).astype(BF16)
+    pair_grad_ref[...] = (grad_mid_ref[...] + back).T
 
 
 def blocks(x, outer, inner, size, wide):
@@ -203,35 +219,76 @@
     first_out_ref[...] = first
     second_out_ref[...] = second
     out = blocks(dot(first, second, 1, 1), wide, size, size, wide).astype(BF16)
-    send_halves(out, sent_ref)
-
-
-def multiply_back(size, wide, got_ref, first_ref, second_ref, sent_ref, scratch):
+    half = sent_ref.shape[2]
+    sent_ref[:, 0, :] = out[:, :half]
+    sent_ref[:, 1, :] = out[:, half:]
+
+
+def multiply_back(size, wide, got_ref, first_ref, second_ref, *refs):
+    sent_ref, scratch = refs[0], refs[-1]
     part = sent_ref.shape[0] // size
-    got = jnp.concatenate([got_ref[:, 0, :].astype(F32), got_ref[:, 1, :].astype(F32)], axis=1)
+    got = [got_ref[:, k, :].astype(F32) for k in range(2)]
+    half = wide * wide // 2
+    if len(refs) > 2:
+        sums = [jnp.sum(x[:, half:], axis=0, keepdims=True) for x in got]
+        empty = jnp.zeros((refs[1].shape[0] - len(sums), sums[0].shape[1]), F32)
+        refs[1][...] = jnp.concatenate(sums + [empty], axis=0).astype(BF16)
+    got = jnp.concatenate([x[:, :half] for x in got], axis=1)
     grad = blocks(got, size, wide, size, wide).astype(BF16)
     sent_ref[:, 0, :] = blocks(dot(grad, second_ref[...], 1, 0), wide, part, size, wide).astype(BF16)
     scratch[...] = dot(grad, first_ref[...], 0, 0)
     sent_ref[:, 1, :] = blocks(reorder(scratch, size, wide), wide, part, size, wide).astype(BF16)
 
 
-def sum_and_spread(got_ref, sent_ref):
-    total = got_ref[0].astype(F32)
-    for i in range(1, got_ref.shape[0]):
-        total += got_ref[i].astype(F32)
-    total = total.astype(BF16)
+def total_of(refs):
+    total = refs[0].astype(F32)
+    for ref in refs[1:]:
+        total += ref.astype(F32)
+    return total.astype(BF16)
+
+
+def sum_near(got_ref, slice_ref, sent_ref):
+    rows = got_ref.shape[1]
+    total = total_of([got_ref[i] for i in range(got_ref.shape[0])])
+    wide = slice_ref.shape[1]
+    for i in range(sent_ref.shape[0]):
+        sent_ref[i, :rows, :] = total
+        sent_ref[i, rows:, :wide] = slice_ref[...]
+        sent_ref[i, rows:, wide:] = jnp.zeros((slice_ref.shape[0], sent_ref.shape[2] - wide), BF16)
+
+
+def sum_far(got_ref, sent_ref):
+    count = got_ref.shape[0]
+    rows = sent_ref.shape[1] - 2 * count
+    total = total_of([got_ref[i, :rows, :] for i in range(count)]).astype(F32)
+    slices = [got_ref[i, rows:, :].astype(F32)[:2] for i in range(count)]
+    total = jnp.concatenate([total] + slices, axis=0).astype(BF16)
     for i in range(sent_ref.shape[0]):
         sent_ref[i] = total
 
 
-def unpack(scale, got_ref, *out_refs):
-    at = 0
-    for ref in out_refs:
-        c = got_ref.shape[1]
-        rows = ref.shape[0]
-        for lane in range(0, ref.shape[1], c):
-            ref[:, lane : lane + c] = got_ref[at : at + rows, :].astype(F32) * scale
-            at += rows
+def unpack(scale, far, wide, got_ref, win1_ref, wout1_ref, win2_ref, wout2_ref):
+    near, rows, c = got_ref.shape
+    rows -= 2 * far
+    flat = jnp.concatenate([got_ref[i, :rows, :] for i in range(near)], axis=0).astype(F32) * scale
+    win_rows = win1_ref.shape[1]
+    for at in range(0, win_rows, c):
+        win1_ref[:, at : at + c] = flat[at : at + c]
+    h = wout1_ref.shape[0]
+    wout1_ref[...] = flat[win_rows : win_rows + h]
+    wout2_ref[...] = flat[win_rows + h :]
+    size = near // SPLIT
+    blocks_of = win_rows // wide // SPLIT
+    run = far // blocks_of
+    for k in range(2):
+        for r in range(run):
+            pieces = []
+            for a in range(SPLIT):
+                for b in range(blocks_of):
+                    at = rows + (b * run + r) * 2 + k
+                    pieces.append(got_ref[a * size : (a + 1) * size, at, :].astype(F32)[:, :wide])
+            at = (k * run + r) * size
+            win2_ref[at : at + size, :] = jnp.concatenate(pieces, axis=1) * scale
 
 
 def call(body, outs, *args, scratch=None):
@@ -271,14 +328,16 @@
         )
         return exchange(sent, everyone), first, second
 
-    def product_back(sent, first, second, group, everyone):
-        sent, = call(
-            functools.partial(multiply_back, size, n), [near], exchange(sent, everyone), first, second, scratch=k_shape
+    def product_back(sent, first, second, group, everyone, *extra):
+        sent, *rest = call(
+            functools.partial(multiply_back, size, n), [near, *extra],
+            exchange(sent, everyone), first, second, scratch=k_shape,
         )
-        return exchange(sent, group)
-
-    one = (("col_lo",) + ROW, COL + ROW)
-    two = (("row_lo",) + COL, ROW + COL)
+        return (exchange(sent, group), *rest)
+
+    one = (("col_a", "col_b") + ROW, COL + ROW)
+    two = (("row_a", "row_b") + COL, ROW + COL)
+    slice_wide = wide * c // (2 * size * size)
 
     sent, proj1, pair_t = call(start_one, [near, ((wide, cells), F32), cell_array], pair, w_in_out)
     got, first1, second1 = product(sent, *one)
@@ -293,37 +352,36 @@
         [((n, n, c), F32), all_devices, cell_array, ((h, c), F32)],
         got, mid_t, proj2, grad_out, w_out_in, scratch=(cells, c),
     )
-    got = product_back(sent, first2, second2, *two)
-    sent, grad_gate1, grad_mid, grad_win_in, grad_wout_out = call(
+    got, = product_back(sent, first2, second2, *two)
+    sent, grad_gate1, grad_mid, grad_wout_out = call(
         between,
-        [all_devices, cell_array, cell_array, ((wide, c), F32), ((h, c), F32)],
+        [((size * size, 2, cells // 2 + slice_wide), BF16), cell_array, cell_array, ((h, c), F32)],
         got, mid_t, proj2, grad_gate2, w_in_in, grad_out, mixed1, proj1, w_out_out, scratch=(cells, c),
     )
-    got = product_back(sent, first1, second1, *one)
-    weight_rows = 2 * (wide + h)
+    got, win2_slice = product_back(sent, first1, second1, *one, ((8, slice_wide), BF16))
+    near_count, far_count = lax.axis_size(NEAR), lax.axis_size(FAR)
+    weight_rows = wide + 2 * h
     pair_grad, weights = call(
         last,
         [((cells, c), F32), ((weight_rows, c), BF16)],
-        got, pair_t, proj1, grad_gate1, w_in_out, grad_mid, grad_win_in, grad_wout_in, grad_wout_out,
-        scratch=(wide, c),
-    )
-
-    near_count, far_count = lax.axis_size(NEAR), lax.axis_size(FAR)
+        got, pair_t, proj1, grad_gate1, w_in_out, grad_mid, grad_wout_out, grad_wout_in,
+    )
+
     each = weight_rows // near_count
     got = exchange(weights.reshape(near_count, each, c), NEAR)
-    sent, = call(sum_and_spread, [((far_count, each, c), BF16)], got)
-    sent, = call(sum_and_spread, [((near_count, each, c), BF16)], exchange(sent, FAR))
+    sent, = call(sum_near, [((far_count, each + 8, c), BF16)], got, win2_slice)
+    sent, = call(sum_far, [((near_count, each + 2 * far_count, c), BF16)], exchange(sent, FAR))
     outs = call(
-        functools.partial(unpack, 1.0 / (n * size)),
+        functools.partial(unpack, 1.0 / (n * size), far_count, slice_wide),
         [((c, wide), F32), ((h, c), F32), ((c, wide), F32), ((h, c), F32)],
-        exchange(sent, NEAR).reshape(weight_rows, c),
+        exchange(sent, NEAR),
     )
     return (pair_new, pair_grad.reshape(n, n, c), *outs)
 
 
 def solution(mesh):
-    rows, cols = mesh.devices.shape
-    fine = Mesh(mesh.devices.reshape(PARTS, rows // PARTS, 2, PARTS // 2, cols // PARTS), ROW + COL)
+    rows, cols = (size // (SPLIT * PARTS) for size in mesh.devices.shape)
+    fine = Mesh(mesh.devices.reshape(SPLIT, PARTS, rows, SPLIT, PARTS, cols), ROW + COL)
     cell = P(ROW, COL, None)
     return jax.shard_map(
         local,

time: 221 us -> 212 us (0.959)
  blocking collectives: 205 us -> 197 us
    all_to_all x11, blocking collectives: 205 us -> 197 us  [exchange(): return lax.all_to_all(x, axes, 0, 0, tiled=True)]
where the time goes in v3:
time: 212 us
  blocking collectives  197 us (93%)
  Pallas kernels  12.1 us (6%)
    all_to_all x11, blocking collectives, exchange(): return lax.all_to_all(x, axes, 0, 0, tiled=True)  197 us
    pallas_call x12, Pallas kernels, call(): pl.pallas_call(body, out_shape=[jax.ShapeDtypeStruct(s, t) for s, t in ou...  12.1 us

profile of v3, /device:TPU:1, one launch (start us, length us, event | category | flops | bytes accessed | tf_op | source)
XLA Modules:
  0.0 211.8 jit_solution(1432797396719231708)
XLA Ops:
  0.6 0.0 copy-start.2
  0.6 0.9 copy-done.2
  1.5 0.0 copy-start.4
  1.5 1.0 copy-done.4
  2.5 0.5 shard_map.109
  3.0 19.0 %all_to_all.55.got_ref = bf16[64,2,576]{2,1,0:T(2,128)(2,1)S(1)} all-to-all(bf16[64,2,576]{2,1,0:T(2,128)(2,1)S(1)} %get-tuple-element.35), channel_id=1, replica_groups=mesh['row_a'=2,'row_q'=4,'row_b'=2,'col_a'=2,'col_q'=4,'col_b'=2] {'col_..., dimensions={0} | all-to-all | bytes 294912 | tf_op jit(solution)/shard_map/all_to_all | solution.py:304
  21.9 1.6 shard_map.110
  23.5 0.0 copy-start.1
  23.6 0.0 copy-start.5
  23.6 28.2 %all_to_all.56.got_ref = bf16[256,2,288]{2,1,0:T(2,128)(2,1)S(1)} all-to-all(bf16[256,2,288]{2,1,0:T(2,128)(2,1)S(1)} %get-tuple-element.36), channel_id=1, replica_groups=mesh['row_a'=2,'row_q'=4,'row_b'=2,'col_a'=2,'col_q'=4,'col_b'=2] {'col_..., dimensions={0} | all-to-all | bytes 589824 | tf_op jit(solution)/shard_map/all_to_all | solution.py:304
  51.8 0.0 copy-done.1
  51.8 0.0 copy-done.5
  51.8 1.0 shard_map.111
  52.7 15.9 %all_to_all.57.got_ref = bf16[64,2,576]{2,1,0:T(2,128)(2,1)S(1)} all-to-all(bf16[64,2,576]{2,1,0:T(2,128)(2,1)S(1)} %get-tuple-element.39), channel_id=1, replica_groups=mesh['row_a'=2,'row_q'=4,'row_b'=2,'col_a'=2,'col_q'=4,'col_b'=2] {'row_..., dimensions={0} | all-to-all | bytes 294912 | tf_op jit(solution)/shard_map/all_to_all | solution.py:304
  68.6 1.6 shard_map.112
  70.2 0.0 copy-start
  70.2 0.0 copy-start.6
  70.2 23.5 %all_to_all.58.got_ref = bf16[256,2,288]{2,1,0:T(2,128)(2,1)S(1)} all-to-all(bf16[256,2,288]{2,1,0:T(2,128)(2,1)S(1)} %get-tuple-element.40), channel_id=1, replica_groups=mesh['row_a'=2,'row_q'=4,'row_b'=2,'col_a'=2,'col_q'=4,'col_b'=2] {'row_..., dimensions={0} | all-to-all | bytes 589824 | tf_op jit(solution)/shard_map/all_to_all | solution.py:304
  93.7 0.0 copy-done
  93.7 0.0 copy-done.6
  93.8 1.2 shard_map.113
  95.0 23.8 %all_to_all.59.got_ref = bf16[256,2,288]{2,1,0:T(2,128)(2,1)S(1)} all-to-all(bf16[256,2,288]{2,1,0:T(2,128)(2,1)S(1)} %get-tuple-element.44), channel_id=1, replica_groups=mesh['row_a'=2,'row_q'=4,'row_b'=2,'col_a'=2,'col_q'=4,'col_b'=2] {'row_..., dimensions={0} | all-to-all | bytes 589824 | tf_op jit(solution)/shard_map/all_to_all | solution.py:304
  118.8 1.2 shard_map.114
  120.0 15.5 %all_to_all.60.got_ref = bf16[64,2,576]{2,1,0:T(2,128)(2,1)S(1)} all-to-all(bf16[64,2,576]{2,1,0:T(2,128)(2,1)S(1)} %shard_map.114), channel_id=1, replica_groups=mesh['row_a'=2,'row_q'=4,'row_b'=2,'col_a'=2,'col_q'=4,'col_b'=2] {'row_..., dimensions={0} | all-to-all | bytes 294912 | tf_op jit(solution)/shard_map/all_to_all | solution.py:304
  135.6 1.4 shard_map.115
  136.9 23.1 %all_to_all.61.got_ref = bf16[256,2,384]{2,1,0:T(2,128)(2,1)S(1)} all-to-all(bf16[256,2,384]{2,1,0:T(2,128)(2,1)S(1)} %get-tuple-element.49), channel_id=1, replica_groups=mesh['row_a'=2,'row_q'=4,'row_b'=2,'col_a'=2,'col_q'=4,'col_b'=2] {'col_..., dimensions={0} | all-to-all | bytes 786432 | tf_op jit(solution)/shard_map/all_to_all | solution.py:304
  160.1 1.3 shard_map.116
  161.4 0.0 copy-start.3
  161.4 12.9 %all_to_all.62.got_ref = bf16[64,2,576]{2,1,0:T(2,128)(2,1)S(1)} all-to-all(bf16[64,2,576]{2,1,0:T(2,128)(2,1)S(1)} %get-tuple-element.52), channel_id=1, replica_groups=mesh['row_a'=2,'row_q'=4,'row_b'=2,'col_a'=2,'col_q'=4,'col_b'=2] {'col_..., dimensions={0} | all-to-all | bytes 294912 | tf_op jit(solution)/shard_map/all_to_all | solution.py:304
  174.3 0.0 copy-done.3
  174.3 1.3 shard_map.117
  175.7 11.5 %all_to_all.63.got_ref = bf16[32,16,128]{2,1,0:T(8,128)(2,1)S(1)} all-to-all(bf16[32,16,128]{2,1,0:T(8,128)(2,1)S(1)} %bitcast.7), channel_id=1, replica_groups=mesh['row_a'=2,'row_q'=4,'row_b'=2,'col_a'=2,'col_q'=4,'col_b'=2] {'col_..., dimensions={0} | all-to-all | bytes 262144 | tf_op jit(solution)/shard_map/all_to_all | solution.py:304
  187.2 9.7 %all_to_all.64.got_ref = bf16[8,24,128]{2,1,0:T(8,128)(2,1)S(1)} all-to-all(bf16[8,24,128]{2,1,0:T(8,128)(2,1)S(1)} %shard_map.118), channel_id=1, replica_groups=mesh['row_a'=2,'row_q'=4,'row_b'=2,'col_a'=2,'col_q'=4,'col_b'=2] {'col_..., dimensions={0} | all-to-all | bytes 98304 | tf_op jit(solution)/shard_map/all_to_all | solution.py:304
  196.9 13.9 %all_to_all.65.got_ref = bf16[32,32,128]{2,1,0:T(8,128)(2,1)S(1)} all-to-all(bf16[32,32,128]{2,1,0:T(8,128)(2,1)S(1)} %shard_map.119), channel_id=1, replica_groups=mesh['row_a'=2,'row_q'=4,'row_b'=2,'col_a'=2,'col_q'=4,'col_b'=2] {'col_..., dimensions={0} | all-to-all | bytes 524288 | tf_op jit(solution)/shard_map/all_to_all | solution.py:304
  210.8 1.0 shard_map.120
  (2 shorter events, 0.1 us)
Async XLA Ops:
  0.6 0.9 copy-start.2
  1.5 1.0 copy-start.4
  23.5 28.2 %copy-start.1 = (bf16[128,384]{1,0:T(8,128)(2,1)S(1)}, bf16[128,384]{1,0:T(8,128)(2,1)}, u32[]{:S(2)}) copy-start(bf16[128,384]{1,0:T(8,128)(2,1)} %w_in_ref.4) | copy-start | bytes 294916
  23.6 28.2 %copy-start.5 = (bf16[64,128]{1,0:T(8,128)(2,1)S(1)}, bf16[64,128]{1,0:T(8,128)(2,1)}, u32[]{:S(2)}) copy-start(bf16[64,128]{1,0:T(8,128)(2,1)} %w_out_ref.5) | copy-start | bytes 49156
  70.2 23.6 %copy-start = (f32[24,24,128]{2,1,0:T(8,128)S(1)}, f32[24,24,128]{2,1,0:T(8,128)}, u32[]{:S(2)}) copy-start(f32[24,24,128]{2,1,0:T(8,128)} %param.7) | copy-start | bytes 884740
  70.2 23.5 %copy-start.6 = (bf16[64,128]{1,0:T(8,128)(2,1)S(1)}, bf16[64,128]{1,0:T(8,128)(2,1)}, u32[]{:S(2)}) copy-start(bf16[64,128]{1,0:T(8,128)(2,1)} %w_out_ref.4) | copy-start | bytes 49156
  161.4 13.0 %copy-start.3 = (bf16[128,384]{1,0:T(8,128)(2,1)S(1)}, bf16[128,384]{1,0:T(8,128)(2,1)}, u32[]{:S(2)}) copy-start(bf16[128,384]{1,0:T(8,128)(2,1)} %w_in_ref.5) | copy-start | bytes 294916

commit v4 on v3

--- a/solution.py
+++ b/solution.py
@@ -15,8 +15,8 @@
 SPLIT = 2
 ROW = ("row_a", "row_q", "row_b")
 COL = ("col_a", "col_q", "col_b")
-NEAR = ("col_a",) + ROW
-FAR = ("col_q", "col_b")
+NEAR = ROW
+FAR = COL
 
 
 def dot(a, b, ca, cb):
@@ -41,10 +41,9 @@
     return jnp.concatenate([ref[pl.ds(j, n, stride=n), :] for j in range(n)], axis=0)
 
 
-def project(x, w_in, proj_ref, sent_ref, order):
+def project(normed, w_in, proj_ref, sent_ref, order):
     h = sent_ref.shape[0]
-    normed, _ = norm(x)
-    proj = dot(w_in, normed.astype(BF16), 0, 0)
+    proj = dot(w_in, normed, 0, 0)
     proj_ref[...] = proj
     for at, place in zip((0, 2 * h), order):
         gated = jax.nn.sigmoid(proj[at + h : at + 2 * h]) * proj[at : at + h]
@@ -103,10 +102,14 @@
     return jnp.concatenate([total(0), total(1)], axis=1)
 
 
-def start_one(pair_ref, w_ref, sent_ref, proj_ref, pair_t_ref):
+def turn_pair(pair_ref, pair_t_ref, normed_ref):
     x = pair_ref[...].T
     pair_t_ref[...] = x
-    project(x, w_ref[...], proj_ref, sent_ref, (0, 1))
+    normed_ref[...] = norm(x)[0].astype(BF16)
+
+
+def start_one(normed_ref, w_ref, sent_ref, proj_ref):
+    project(normed_ref[...], w_ref[...], proj_ref, sent_ref, (0, 1))
 
 
 def middle(
@@ -121,7 +124,7 @@
     scratch[...] = mid.T
     mid = swap_cells(scratch, int(round(scratch.shape[0] ** 0.5))).T
     mid_ref[...] = mid
-    project(mid, w_in_ref[...], proj2_ref, sent_ref, (1, 0))
+    project(norm(mid)[0].astype(BF16), w_in_ref[...], proj2_ref, sent_ref, (1, 0))
 
 
 def turn(
@@ -207,18 +210,50 @@
     return jnp.concatenate(rows, axis=0)
 
 
+def blocks_low(x, outer, inner, size, wide):
+    lanes = 128
+    width = -(-wide * (outer + inner) // lanes) * lanes
+    lane = lax.broadcasted_iota(jnp.int32, (size, lanes), 1)
+
+    def masks(diagonal):
+        low, high = diagonal * wide, (diagonal + 1) * wide
+        return [
+            (t, (lane >= low - t * lanes) & (lane < high - t * lanes))
+            for t in range(low // lanes, (high - 1) // lanes + 1)
+        ]
+
+    chosen = [masks(diagonal) for diagonal in range(outer + inner - 1)]
+    empty = jnp.zeros((size, width - inner * wide), x.dtype)
+    turned = []
+    for o in range(outer):
+        row = jnp.concatenate([x[o * size : (o + 1) * size], empty], axis=1)
+        turned.append(pltpu.roll(row, o * wide, 1) if o else row)
+    rows = []
+    for r in range(inner):
+        merged = [None] * (width // lanes)
+        for o in range(outer):
+            for t, mask in chosen[r + o]:
+                piece = turned[o][:, t * lanes : (t + 1) * lanes]
+                merged[t] = piece if merged[t] is None else jnp.where(mask, piece, merged[t])
+        zero = jnp.zeros((size, lanes), x.dtype)
+        row = jnp.concatenate([zero if m is None else m for m in merged], axis=1)
+        row = pltpu.roll(row, width - r * wide, 1) if r else row
+        rows.append(row[:, : outer * wide])
+    return jnp.concatenate(rows, axis=0)
+
+
 def reorder(ref, outer, inner):
     return jnp.concatenate([ref[pl.ds(r, outer, stride=inner), :] for r in range(inner)], axis=0)
 
 
 def multiply(size, wide, got_ref, sent_ref, first_out_ref, second_out_ref, scratch):
     part = got_ref.shape[0] // size
-    first = blocks(got_ref[:, 0, :].astype(F32), part, wide, size, wide).astype(BF16)
-    scratch[...] = blocks(got_ref[:, 1, :].astype(F32), part, wide, size, wide)
+    first = blocks_low(got_ref[:, 0, :], part, wide, size, wide)
+    scratch[...] = blocks_low(got_ref[:, 1, :], part, wide, size, wide).astype(F32)
     second = reorder(scratch, wide, size).astype(BF16)
     first_out_ref[...] = first
     second_out_ref[...] = second
-    out = blocks(dot(first, second, 1, 1), wide, size, size, wide).astype(BF16)
+    out = blocks_low(dot(first, second, 1, 1).astype(BF16), wide, size, size, wide)
     half = sent_ref.shape[2]
     sent_ref[:, 0, :] = out[:, :half]
     sent_ref[:, 1, :] = out[:, half:]
@@ -267,9 +302,10 @@
         sent_ref[i] = total
 
 
-def unpack(scale, far, wide, got_ref, win1_ref, wout1_ref, win2_ref, wout2_ref):
+def unpack(scale, far, wide, got_ref, win1_ref, wout1_ref, win2_ref, wout2_ref, scratch):
     near, rows, c = got_ref.shape
     rows -= 2 * far
+    scratch[...] = got_ref[:, rows:, :].reshape(scratch.shape).astype(F32)
     flat = jnp.concatenate([got_ref[i, :rows, :] for i in range(near)], axis=0).astype(F32) * scale
     win_rows = win1_ref.shape[1]
     for at in range(0, win_rows, c):
@@ -277,18 +313,14 @@
     h = wout1_ref.shape[0]
     wout1_ref[...] = flat[win_rows : win_rows + h]
     wout2_ref[...] = flat[win_rows + h :]
-    size = near // SPLIT
-    blocks_of = win_rows // wide // SPLIT
-    run = far // blocks_of
+    run = far // (win_rows // wide)
     for k in range(2):
         for r in range(run):
-            pieces = []
-            for a in range(SPLIT):
-                for b in range(blocks_of):
-                    at = rows + (b * run + r) * 2 + k
-                    pieces.append(got_ref[a * size : (a + 1) * size, at, :].astype(F32)[:, :wide])
-            at = (k * run + r) * size
-            win2_ref[at : at + size, :] = jnp.concatenate(pieces, axis=1) * scale
+            pieces = [
+                scratch[pl.ds((at + r) * 2 + k, near, stride=2 * far), :][:, :wide] for at in range(0, far, run)
+            ]
+            at = (k * run + r) * near
+            win2_ref[at : at + near, :] = jnp.concatenate(pieces, axis=1) * scale
 
 
 def call(body, outs, *args, scratch=None):
@@ -339,7 +371,8 @@
     two = (("row_a", "row_b") + COL, ROW + COL)
     slice_wide = wide * c // (2 * size * size)
 
-    sent, proj1, pair_t = call(start_one, [near, ((wide, cells), F32), cell_array], pair, w_in_out)
+    pair_t, normed1 = call(turn_pair, [cell_array, ((c, cells), BF16)], pair)
+    sent, proj1 = call(start_one, [near, ((wide, cells), F32)], normed1, w_in_out)
     got, first1, second1 = product(sent, *one)
     sent, proj2, mixed1, mid_t = call(
         middle,
@@ -374,7 +407,7 @@
     outs = call(
         functools.partial(unpack, 1.0 / (n * size), far_count, slice_wide),
         [((c, wide), F32), ((h, c), F32), ((c, wide), F32), ((h, c), F32)],
-        exchange(sent, NEAR),
+        exchange(sent, NEAR), scratch=(near_count * 2 * far_count, c),
     )
     return (pair_new, pair_grad.reshape(n, n, c), *outs)
 

time: 212 us -> 210 us (level)
    pallas_call x12 -> x13, Pallas kernels: 12.1 us -> 11.8 us  [call(): pl.pallas_call(body, out_shape=[jax.ShapeDtypeStruct(s, t) for s, t in ou...]
where the time goes in v4:
time: 210 us
  blocking collectives  196 us (93%)
  Pallas kernels  11.8 us (6%)
    all_to_all x11, blocking collectives, exchange(): return lax.all_to_all(x, axes, 0, 0, tiled=True)  196 us
    pallas_call x13, Pallas kernels, call(): pl.pallas_call(body, out_shape=[jax.ShapeDtypeStruct(s, t) for s, t in ou...  11.8 us

profile of v4, /device:TPU:1, one launch (start us, length us, event | category | flops | bytes accessed | tf_op | source)
XLA Modules:
  0.0 209.8 jit_solution(14131459034105878361)
XLA Ops:
  0.6 0.0 copy-start.3
  0.6 1.0 copy-done.3
  1.6 0.0 copy-start.2
  1.6 0.2 shard_map.109
  1.8 0.7 copy-done.2
  2.5 0.4 shard_map.110
  2.9 19.0 %all_to_all.55.got_ref = bf16[64,2,576]{2,1,0:T(2,128)(2,1)S(1)} all-to-all(bf16[64,2,576]{2,1,0:T(2,128)(2,1)S(1)} %get-tuple-element.37), channel_id=1, replica_groups=mesh['row_a'=2,'row_q'=4,'row_b'=2,'col_a'=2,'col_q'=4,'col_b'=2] {'col_..., dimensions={0} | all-to-all | bytes 294912 | tf_op jit(solution)/shard_map/all_to_all | solution.py:336
  21.8 1.4 shard_map.111
  23.2 0.0 copy-start.1
  23.2 0.0 copy-start.4
  23.3 28.2 %all_to_all.56.got_ref = bf16[256,2,288]{2,1,0:T(2,128)(2,1)S(1)} all-to-all(bf16[256,2,288]{2,1,0:T(2,128)(2,1)S(1)} %get-tuple-element.38), channel_id=1, replica_groups=mesh['row_a'=2,'row_q'=4,'row_b'=2,'col_a'=2,'col_q'=4,'col_b'=2] {'col_..., dimensions={0} | all-to-all | bytes 589824 | tf_op jit(solution)/shard_map/all_to_all | solution.py:336
  51.5 0.0 copy-done.1
  51.5 0.0 copy-done.4
  51.5 1.0 shard_map.112
  52.5 15.9 %all_to_all.57.got_ref = bf16[64,2,576]{2,1,0:T(2,128)(2,1)S(1)} all-to-all(bf16[64,2,576]{2,1,0:T(2,128)(2,1)S(1)} %get-tuple-element.41), channel_id=1, replica_groups=mesh['row_a'=2,'row_q'=4,'row_b'=2,'col_a'=2,'col_q'=4,'col_b'=2] {'row_..., dimensions={0} | all-to-all | bytes 294912 | tf_op jit(solution)/shard_map/all_to_all | solution.py:336
  68.3 1.4 shard_map.113
  69.7 0.0 copy-start
  69.7 0.0 copy-start.5
  69.8 23.5 %all_to_all.58.got_ref = bf16[256,2,288]{2,1,0:T(2,128)(2,1)S(1)} all-to-all(bf16[256,2,288]{2,1,0:T(2,128)(2,1)S(1)} %get-tuple-element.42), channel_id=1, replica_groups=mesh['row_a'=2,'row_q'=4,'row_b'=2,'col_a'=2,'col_q'=4,'col_b'=2] {'row_..., dimensions={0} | all-to-all | bytes 589824 | tf_op jit(solution)/shard_map/all_to_all | solution.py:336
  93.3 0.0 copy-done
  93.3 0.0 copy-done.5
  93.3 1.2 shard_map.114
  94.5 23.8 %all_to_all.59.got_ref = bf16[256,2,288]{2,1,0:T(2,128)(2,1)S(1)} all-to-all(bf16[256,2,288]{2,1,0:T(2,128)(2,1)S(1)} %get-tuple-element.46), channel_id=1, replica_groups=mesh['row_a'=2,'row_q'=4,'row_b'=2,'col_a'=2,'col_q'=4,'col_b'=2] {'row_..., dimensions={0} | all-to-all | bytes 589824 | tf_op jit(solution)/shard_map/all_to_all | solution.py:336
  118.3 1.2 shard_map.115
  119.6 15.5 %all_to_all.60.got_ref = bf16[64,2,576]{2,1,0:T(2,128)(2,1)S(1)} all-to-all(bf16[64,2,576]{2,1,0:T(2,128)(2,1)S(1)} %shard_map.115), channel_id=1, replica_groups=mesh['row_a'=2,'row_q'=4,'row_b'=2,'col_a'=2,'col_q'=4,'col_b'=2] {'row_..., dimensions={0} | all-to-all | bytes 294912 | tf_op jit(solution)/shard_map/all_to_all | solution.py:336
  135.1 1.4 shard_map.116
  136.5 23.1 %all_to_all.61.got_ref = bf16[256,2,384]{2,1,0:T(2,128)(2,1)S(1)} all-to-all(bf16[256,2,384]{2,1,0:T(2,128)(2,1)S(1)} %get-tuple-element.51), channel_id=1, replica_groups=mesh['row_a'=2,'row_q'=4,'row_b'=2,'col_a'=2,'col_q'=4,'col_b'=2] {'col_..., dimensions={0} | all-to-all | bytes 786432 | tf_op jit(solution)/shard_map/all_to_all | solution.py:336
  159.6 1.3 shard_map.117
  160.9 12.8 %all_to_all.62.got_ref = bf16[64,2,576]{2,1,0:T(2,128)(2,1)S(1)} all-to-all(bf16[64,2,576]{2,1,0:T(2,128)(2,1)S(1)} %get-tuple-element.54), channel_id=1, replica_groups=mesh['row_a'=2,'row_q'=4,'row_b'=2,'col_a'=2,'col_q'=4,'col_b'=2] {'col_..., dimensions={0} | all-to-all | bytes 294912 | tf_op jit(solution)/shard_map/all_to_all | solution.py:336
  173.7 1.3 shard_map.118
  175.0 8.9 %all_to_all.63.got_ref = bf16[16,32,128]{2,1,0:T(8,128)(2,1)S(1)} all-to-all(bf16[16,32,128]{2,1,0:T(8,128)(2,1)S(1)} %bitcast.7), channel_id=1, replica_groups=mesh['row_a'=2,'row_q'=4,'row_b'=2,'col_a'=2,'col_q'=4,'col_b'=2] {'row_..., dimensions={0} | all-to-all | bytes 262144 | tf_op jit(solution)/shard_map/all_to_all | solution.py:336
  184.0 13.0 %all_to_all.64.got_ref = bf16[16,40,128]{2,1,0:T(8,128)(2,1)S(1)} all-to-all(bf16[16,40,128]{2,1,0:T(8,128)(2,1)S(1)} %shard_map.119), channel_id=1, replica_groups=mesh['row_a'=2,'row_q'=4,'row_b'=2,'col_a'=2,'col_q'=4,'col_b'=2] {'col_..., dimensions={0} | all-to-all | bytes 327680 | tf_op jit(solution)/shard_map/all_to_all | solution.py:336
  197.1 11.8 %all_to_all.65.got_ref = bf16[16,64,128]{2,1,0:T(8,128)(2,1)S(1)} all-to-all(bf16[16,64,128]{2,1,0:T(8,128)(2,1)S(1)} %shard_map.120), channel_id=1, replica_groups=mesh['row_a'=2,'row_q'=4,'row_b'=2,'col_a'=2,'col_q'=4,'col_b'=2] {'row_..., dimensions={0} | all-to-all | bytes 524288 | tf_op jit(solution)/shard_map/all_to_all | solution.py:336
  208.8 0.9 shard_map.121
  (2 shorter events, 0.1 us)
Async XLA Ops:
  0.6 1.0 copy-start.3
  1.6 0.9 copy-start.2
  23.2 28.2 %copy-start.1 = (bf16[128,384]{1,0:T(8,128)(2,1)S(1)}, bf16[128,384]{1,0:T(8,128)(2,1)}, u32[]{:S(2)}) copy-start(bf16[128,384]{1,0:T(8,128)(2,1)} %w_in_ref.4) | copy-start | bytes 294916
  23.2 28.2 %copy-start.4 = (bf16[64,128]{1,0:T(8,128)(2,1)S(1)}, bf16[64,128]{1,0:T(8,128)(2,1)}, u32[]{:S(2)}) copy-start(bf16[64,128]{1,0:T(8,128)(2,1)} %w_out_ref.5) | copy-start | bytes 49156
  69.7 23.5 %copy-start = (f32[24,24,128]{2,1,0:T(8,128)S(1)}, f32[24,24,128]{2,1,0:T(8,128)}, u32[]{:S(2)}) copy-start(f32[24,24,128]{2,1,0:T(8,128)} %param.7) | copy-start | bytes 884740
  69.7 23.5 %copy-start.5 = (bf16[64,128]{1,0:T(8,128)(2,1)S(1)}, bf16[64,128]{1,0:T(8,128)(2,1)}, u32[]{:S(2)}) copy-start(bf16[64,128]{1,0:T(8,128)(2,1)} %w_out_ref.4) | copy-start | bytes 49156

commit v5 on v4

--- a/solution.py
+++ b/solution.py
@@ -11,6 +11,8 @@
 EPS = 1e-05
 F32 = jnp.float32
 BF16 = jnp.bfloat16
+TILE = 128
+PAIRS = (1536, TILE)
 PARTS = 4
 SPLIT = 2
 ROW = ("row_a", "row_q", "row_b")
@@ -37,17 +39,50 @@
     )
 
 
+def read_pairs(ref, scratch):
+    count, _, lanes = ref.shape
+    rows = [], []
+    for tile in range(-(-lanes // TILE)):
+        low, high = tile * TILE, min(lanes, (tile + 1) * TILE)
+        x = ref[:, :, low:high]
+        if high - low < TILE:
+            x = jnp.concatenate([x, jnp.zeros((count, 2, TILE - (high - low)), x.dtype)], axis=2)
+        at = tile * 2 * count
+        scratch[at : at + 2 * count, :] = x.reshape(2 * count, TILE).astype(F32)
+        for k in range(2):
+            rows[k].append(scratch[pl.ds(at + k, count, stride=2), :][:, : high - low])
+    return [jnp.concatenate(x, axis=1) for x in rows]
+
+
+def write_pairs(ref, pair, scratch):
+    count, _, lanes = ref.shape
+    for tile in range(-(-lanes // TILE)):
+        low, high = tile * TILE, min(lanes, (tile + 1) * TILE)
+        at = tile * 2 * count
+        for k in range(2):
+            x = pair[k][:, low:high]
+            if high - low < TILE:
+                x = jnp.concatenate([x, jnp.zeros((count, TILE - (high - low)), F32)], axis=1)
+            scratch[pl.ds(at + k, count, stride=2), :] = x
+        x = scratch[at : at + 2 * count, :].astype(BF16).reshape(count, 2, TILE)
+        ref[:, :, low:high] = x[:, :, : high - low]
+
+
+def write_plain(ref, pair):
+    for k in range(2):
+        ref[:, k, :] = pair[k].astype(BF16)
+
+
 def swap_cells(ref, n):
     return jnp.concatenate([ref[pl.ds(j, n, stride=n), :] for j in range(n)], axis=0)
 
 
-def project(normed, w_in, proj_ref, sent_ref, order):
+def project(normed, w_in, proj_ref, sent_ref, order, pairs_out):
     h = sent_ref.shape[0]
     proj = dot(w_in, normed, 0, 0)
     proj_ref[...] = proj
-    for at, place in zip((0, 2 * h), order):
-        gated = jax.nn.sigmoid(proj[at + h : at + 2 * h]) * proj[at : at + h]
-        sent_ref[:, place, :] = gated.astype(BF16)
+    gated = [jax.nn.sigmoid(proj[at + h : at + 2 * h]) * proj[at : at + h] for at in (0, 2 * h)]
+    write_plain(sent_ref, [gated[place] for place in order])
 
 
 def project_back(x, proj_ref, w_in, gl, gr, grad_gate):
@@ -91,7 +126,6 @@
 def summed(got_ref):
     count = got_ref.shape[0]
     h = count // PARTS
-
     def total(k):
         sums = {}
         for at, channel, run in owners(count, h):
@@ -102,19 +136,26 @@
     return jnp.concatenate([total(0), total(1)], axis=1)
 
 
+def to_owners(x):
+    h, cells = x.shape
+    runs = [x[channel : channel + run] for _, channel, run in owners(PARTS * h, h)]
+    x = jnp.concatenate(runs, axis=0)
+    return [x[:, : cells // 2], x[:, cells // 2 :]]
+
+
 def turn_pair(pair_ref, pair_t_ref, normed_ref):
     x = pair_ref[...].T
     pair_t_ref[...] = x
     normed_ref[...] = norm(x)[0].astype(BF16)
 
 
-def start_one(normed_ref, w_ref, sent_ref, proj_ref):
-    project(normed_ref[...], w_ref[...], proj_ref, sent_ref, (0, 1))
+def start_one(normed_ref, w_ref, sent_ref, proj_ref, pairs_out):
+    project(normed_ref[...], w_ref[...], proj_ref, sent_ref, (0, 1), pairs_out)
 
 
 def middle(
     got_ref, pair_t_ref, proj1_ref, w_out_ref, w_in_ref,
-    sent_ref, proj2_ref, mixed_ref, mid_ref, scratch,
+    sent_ref, proj2_ref, mixed_ref, mid_ref, scratch, pairs_out,
 ):
     h = sent_ref.shape[0]
     mixed = summed(got_ref)
@@ -124,12 +165,12 @@
     scratch[...] = mid.T
     mid = swap_cells(scratch, int(round(scratch.shape[0] ** 0.5))).T
     mid_ref[...] = mid
-    project(norm(mid)[0].astype(BF16), w_in_ref[...], proj2_ref, sent_ref, (1, 0))
+    project(norm(mid)[0].astype(BF16), w_in_ref[...], proj2_ref, sent_ref, (1, 0), pairs_out)
 
 
 def turn(
     got_ref, mid_ref, proj_ref, grad_out_ref, w_out_ref,
-    new_ref, sent_ref, grad_gate_ref, grad_w_ref, scratch,
+    new_ref, sent_ref, grad_gate_ref, grad_w_ref, scratch, pairs_out,
 ):
     h = got_ref.shape[0] // PARTS
     n = new_ref.shape[0]
@@ -140,23 +181,19 @@
     new_ref[...] = swap_cells(scratch, n).reshape(new_ref.shape)
     grad_new = swap_cells(grad_out_ref, n).T
     grad, grad_gate, grad_w = finish_back(grad_new, gate, out, normed, rstd, post, w_out_ref[...])
-    grad = grad.astype(BF16)
-    half = sent_ref.shape[2]
-    for at, channel, run in owners(sent_ref.shape[0], h):
-        for k in range(2):
-            sent_ref[at : at + run, k, :] = grad[channel : channel + run, k * half : (k + 1) * half]
+    write_plain(sent_ref, to_owners(grad))
     grad_gate_ref[...] = grad_gate
     grad_w_ref[...] = grad_w
 
 
 def between(
     got_ref, mid_ref, proj2_ref, grad_gate2_ref, w_in_ref, grad_out_ref, mixed_ref, proj1_ref, w_out_ref,
-    sent_ref, grad_gate_ref, grad_mid_ref, grad_wout_ref, scratch,
+    sent_ref, grad_gate_ref, grad_mid_ref, grad_wout_ref, scratch, pairs_out,
 ):
     h, _, cells = got_ref.shape
+    grad_right, grad_left = (got_ref[:, k, :].astype(F32) for k in range(2))
     back, low, grad_proj = project_back(
-        mid_ref[...], proj2_ref, w_in_ref[...], got_ref[:, 1, :].astype(F32), got_ref[:, 0, :].astype(F32),
-        grad_gate2_ref[...],
+        mid_ref[...], proj2_ref, w_in_ref[...], grad_left, grad_right, grad_gate2_ref[...]
     )
     scratch[...] = back.T
     n = int(round(scratch.shape[0] ** 0.5))
@@ -168,30 +205,25 @@
     grad, grad_gate, grad_w = finish_back(grad_mid, gate, out, normed, rstd, post, w_out)
     grad_gate_ref[...] = grad_gate
     grad_wout_ref[...] = grad_w
-    grad = grad.astype(BF16)
-    half = cells // 2
-    count = sent_ref.shape[0]
-    wide = sent_ref.shape[2] - half
+    wide = sent_ref.shape[2] - cells // 2
     pairs = low.shape[0] // 2
-    weights = [
-        dot(low, grad_proj[at : at + wide], 1, 1).astype(BF16) for at in range(0, grad_proj.shape[0], wide)
+    weights = [dot(low, grad_proj[at : at + wide], 1, 1) for at in range(0, grad_proj.shape[0], wide)]
+    sent = [
+        jnp.concatenate(
+            [x, jnp.concatenate([w[k * pairs : (k + 1) * pairs] for w in weights], axis=0)], axis=1
+        )
+        for k, x in enumerate(to_owners(grad))
     ]
-    for at, channel, run in owners(count, h):
-        block, first = at // pairs, at % pairs
-        for k in range(2):
-            rows = weights[block][k * pairs + first : k * pairs + first + run]
-            sent_ref[at : at + run, k, :] = jnp.concatenate(
-                [grad[channel : channel + run, k * half : (k + 1) * half], rows], axis=1
-            )
+    write_plain(sent_ref, sent)
 
 
 def last(
     got_ref, pair_t_ref, proj_ref, grad_gate_ref, w_in_ref, grad_mid_ref, wout1_ref, wout2_ref,
     pair_grad_ref, weights_ref,
 ):
+    grad_left, grad_right = (got_ref[:, k, :].astype(F32) for k in range(2))
     back, low, grad_proj = project_back(
-        pair_t_ref[...], proj_ref, w_in_ref[...], got_ref[:, 0, :].astype(F32), got_ref[:, 1, :].astype(F32),
-        grad_gate_ref[...],
+        pair_t_ref[...], proj_ref, w_in_ref[...], grad_left, grad_right, grad_gate_ref[...]
     )
     c = low.shape[0]
     rows = [dot(low, grad_proj[at : at + c], 1, 1) for at in range(0, grad_proj.shape[0], c)]
@@ -246,33 +278,34 @@
     return jnp.concatenate([ref[pl.ds(r, outer, stride=inner), :] for r in range(inner)], axis=0)
 
 
-def multiply(size, wide, got_ref, sent_ref, first_out_ref, second_out_ref, scratch):
+def multiply(size, wide, got_ref, sent_ref, first_out_ref, second_out_ref, scratch, pairs_in, pairs_out):
     part = got_ref.shape[0] // size
-    first = blocks_low(got_ref[:, 0, :], part, wide, size, wide)
-    scratch[...] = blocks_low(got_ref[:, 1, :], part, wide, size, wide).astype(F32)
+    first, second = read_pairs(got_ref, pairs_in)
+    first = blocks_low(first.astype(BF16), part, wide, size, wide).astype(BF16)
+    scratch[...] = blocks_low(second.astype(BF16), part, wide, size, wide).astype(F32)
     second = reorder(scratch, wide, size).astype(BF16)
     first_out_ref[...] = first
     second_out_ref[...] = second
-    out = blocks_low(dot(first, second, 1, 1).astype(BF16), wide, size, size, wide)
+    out = blocks_low(dot(first, second, 1, 1).astype(BF16), wide, size, size, wide).astype(F32)
     half = sent_ref.shape[2]
-    sent_ref[:, 0, :] = out[:, :half]
-    sent_ref[:, 1, :] = out[:, half:]
+    write_pairs(sent_ref, [out[:, :half], out[:, half:]], pairs_out)
 
 
 def multiply_back(size, wide, got_ref, first_ref, second_ref, *refs):
-    sent_ref, scratch = refs[0], refs[-1]
+    sent_ref, (scratch, pairs_out) = refs[0], refs[-2:]
     part = sent_ref.shape[0] // size
     got = [got_ref[:, k, :].astype(F32) for k in range(2)]
     half = wide * wide // 2
-    if len(refs) > 2:
+    if len(refs) > 3:
         sums = [jnp.sum(x[:, half:], axis=0, keepdims=True) for x in got]
         empty = jnp.zeros((refs[1].shape[0] - len(sums), sums[0].shape[1]), F32)
         refs[1][...] = jnp.concatenate(sums + [empty], axis=0).astype(BF16)
     got = jnp.concatenate([x[:, :half] for x in got], axis=1)
     grad = blocks(got, size, wide, size, wide).astype(BF16)
-    sent_ref[:, 0, :] = blocks(dot(grad, second_ref[...], 1, 0), wide, part, size, wide).astype(BF16)
+    sent = [blocks(dot(grad, second_ref[...], 1, 0), wide, part, size, wide)]
     scratch[...] = dot(grad, first_ref[...], 0, 0)
-    sent_ref[:, 1, :] = blocks(reorder(scratch, size, wide), wide, part, size, wide).astype(BF16)
+    sent.append(blocks(reorder(scratch, size, wide), wide, part, size, wide))
+    write_plain(sent_ref, sent)
 
 
 def total_of(refs):
@@ -323,11 +356,11 @@
             win2_ref[at : at + near, :] = jnp.concatenate(pieces, axis=1) * scale
 
 
-def call(body, outs, *args, scratch=None):
+def call(body, outs, *args, scratch=()):
     return pl.pallas_call(
         body,
         out_shape=[jax.ShapeDtypeStruct(s, t) for s, t in outs],
-        scratch_shapes=[] if scratch is None else [pltpu.VMEM(scratch, F32)],
+        scratch_shapes=[pltpu.VMEM(shape, F32) for shape in scratch],
         compiler_params=pltpu.CompilerParams(vmem_limit_bytes=16 * 1024 * 1024),
     )(*args)
 
@@ -356,14 +389,14 @@
         sent, first, second = call(
             functools.partial(multiply, size, n),
             [all_devices, (k_shape, BF16), (k_shape, BF16)],
-            exchange(sent, group), scratch=k_shape,
+            exchange(sent, group), scratch=[k_shape, PAIRS, PAIRS],
         )
         return exchange(sent, everyone), first, second
 
     def product_back(sent, first, second, group, everyone, *extra):
         sent, *rest = call(
             functools.partial(multiply_back, size, n), [near, *extra],
-            exchange(sent, everyone), first, second, scratch=k_shape,
+            exchange(sent, everyone), first, second, scratch=[k_shape, PAIRS],
         )
         return (exchange(sent, group), *rest)
 
@@ -372,24 +405,24 @@
     slice_wide = wide * c // (2 * size * size)
 
     pair_t, normed1 = call(turn_pair, [cell_array, ((c, cells), BF16)], pair)
-    sent, proj1 = call(start_one, [near, ((wide, cells), F32)], normed1, w_in_out)
+    sent, proj1 = call(start_one, [near, ((wide, cells), F32)], normed1, w_in_out, scratch=[PAIRS])
     got, first1, second1 = product(sent, *one)
     sent, proj2, mixed1, mid_t = call(
         middle,
         [near, ((wide, cells), F32), (low, F32), cell_array],
-        got, pair_t, proj1, w_out_out, w_in_in, scratch=(cells, c),
+        got, pair_t, proj1, w_out_out, w_in_in, scratch=[(cells, c), PAIRS],
     )
     got, first2, second2 = product(sent, *two)
     pair_new, sent, grad_gate2, grad_wout_in = call(
         turn,
         [((n, n, c), F32), all_devices, cell_array, ((h, c), F32)],
-        got, mid_t, proj2, grad_out, w_out_in, scratch=(cells, c),
+        got, mid_t, proj2, grad_out, w_out_in, scratch=[(cells, c), PAIRS],
     )
     got, = product_back(sent, first2, second2, *two)
     sent, grad_gate1, grad_mid, grad_wout_out = call(
         between,
         [((size * size, 2, cells // 2 + slice_wide), BF16), cell_array, cell_array, ((h, c), F32)],
-        got, mid_t, proj2, grad_gate2, w_in_in, grad_out, mixed1, proj1, w_out_out, scratch=(cells, c),
+        got, mid_t, proj2, grad_gate2, w_in_in, grad_out, mixed1, proj1, w_out_out, scratch=[(cells, c), PAIRS],
     )
     got, win2_slice = product_back(sent, first1, second1, *one, ((8, slice_wide), BF16))
     near_count, far_count = lax.axis_size(NEAR), lax.axis_size(FAR)
@@ -407,7 +440,7 @@
     outs = call(
         functools.partial(unpack, 1.0 / (n * size), far_count, slice_wide),
         [((c, wide), F32), ((h, c), F32), ((c, wide), F32), ((h, c), F32)],
-        exchange(sent, NEAR), scratch=(near_count * 2 * far_count, c),
+        exchange(sent, NEAR), scratch=[(near_count * 2 * far_count, c)],
     )
     return (pair_new, pair_grad.reshape(n, n, c), *outs)
 

time: 210 us -> 210 us (level)
  no operation moved by 1% of the time
where the time goes in v5:
time: 210 us; the launch traced here: 209 us
  blocking collectives  196 us (93%)
  Pallas kernels  11.2 us (5%)
    all_to_all x11, blocking collectives, exchange(): return lax.all_to_all(x, axes, 0, 0, tiled=True)  196 us
    pallas_call x13, Pallas kernels, call(): pl.pallas_call(body, out_shape=[jax.ShapeDtypeStruct(s, t) for s, t in ou...  11.2 us

profile of v5, /device:TPU:1, one launch (start us, length us, event | category | flops | bytes accessed | tf_op | source)
XLA Modules:
  0.0 209.2 jit_solution(446990243726793183)
XLA Ops:
  0.6 0.0 copy-start.3
  0.6 1.0 copy-done.3
  1.6 0.0 copy-start.2
  1.6 0.2 shard_map.109
  1.8 0.7 copy-done.2
  2.5 0.4 shard_map.110
  2.9 19.0 %all_to_all.55.got_ref = bf16[64,2,576]{2,1,0:T(2,128)(2,1)S(1)} all-to-all(bf16[64,2,576]{2,1,0:T(2,128)(2,1)S(1)} %get-tuple-element.37), channel_id=1, replica_groups=mesh['row_a'=2,'row_q'=4,'row_b'=2,'col_a'=2,'col_q'=4,'col_b'=2] {'col_..., dimensions={0} | all-to-all | bytes 294912 | tf_op jit(solution)/shard_map/all_to_all | solution.py:369
  21.8 1.1 shard_map.111
  22.9 0.0 copy-start.1
  22.9 0.0 copy-start.4
  23.0 28.2 %all_to_all.56.got_ref = bf16[256,2,288]{2,1,0:T(2,128)(2,1)S(1)} all-to-all(bf16[256,2,288]{2,1,0:T(2,128)(2,1)S(1)} %get-tuple-element.38), channel_id=1, replica_groups=mesh['row_a'=2,'row_q'=4,'row_b'=2,'col_a'=2,'col_q'=4,'col_b'=2] {'col_..., dimensions={0} | all-to-all | bytes 589824 | tf_op jit(solution)/shard_map/all_to_all | solution.py:369
  51.2 0.0 copy-done.1
  51.2 0.0 copy-done.4
  51.2 1.0 shard_map.112
  52.2 15.9 %all_to_all.57.got_ref = bf16[64,2,576]{2,1,0:T(2,128)(2,1)S(1)} all-to-all(bf16[64,2,576]{2,1,0:T(2,128)(2,1)S(1)} %get-tuple-element.41), channel_id=1, replica_groups=mesh['row_a'=2,'row_q'=4,'row_b'=2,'col_a'=2,'col_q'=4,'col_b'=2] {'row_..., dimensions={0} | all-to-all | bytes 294912 | tf_op jit(solution)/shard_map/all_to_all | solution.py:369
  68.0 1.1 shard_map.113
  69.1 0.0 copy-start
  69.2 0.0 copy-start.5
  69.2 23.5 %all_to_all.58.got_ref = bf16[256,2,288]{2,1,0:T(2,128)(2,1)S(1)} all-to-all(bf16[256,2,288]{2,1,0:T(2,128)(2,1)S(1)} %get-tuple-element.42), channel_id=1, replica_groups=mesh['row_a'=2,'row_q'=4,'row_b'=2,'col_a'=2,'col_q'=4,'col_b'=2] {'row_..., dimensions={0} | all-to-all | bytes 589824 | tf_op jit(solution)/shard_map/all_to_all | solution.py:369
  92.7 0.0 copy-done
  92.7 0.0 copy-done.5
  92.7 1.2 shard_map.114
  93.9 23.8 %all_to_all.59.got_ref = bf16[256,2,288]{2,1,0:T(2,128)(2,1)S(1)} all-to-all(bf16[256,2,288]{2,1,0:T(2,128)(2,1)S(1)} %get-tuple-element.46), channel_id=1, replica_groups=mesh['row_a'=2,'row_q'=4,'row_b'=2,'col_a'=2,'col_q'=4,'col_b'=2] {'row_..., dimensions={0} | all-to-all | bytes 589824 | tf_op jit(solution)/shard_map/all_to_all | solution.py:369
  117.8 1.2 shard_map.115
  119.0 15.6 %all_to_all.60.got_ref = bf16[64,2,576]{2,1,0:T(2,128)(2,1)S(1)} all-to-all(bf16[64,2,576]{2,1,0:T(2,128)(2,1)S(1)} %shard_map.115), channel_id=1, replica_groups=mesh['row_a'=2,'row_q'=4,'row_b'=2,'col_a'=2,'col_q'=4,'col_b'=2] {'row_..., dimensions={0} | all-to-all | bytes 294912 | tf_op jit(solution)/shard_map/all_to_all | solution.py:369
  134.6 1.4 shard_map.116
  136.0 23.0 %all_to_all.61.got_ref = bf16[256,2,384]{2,1,0:T(2,128)(2,1)S(1)} all-to-all(bf16[256,2,384]{2,1,0:T(2,128)(2,1)S(1)} %get-tuple-element.51), channel_id=1, replica_groups=mesh['row_a'=2,'row_q'=4,'row_b'=2,'col_a'=2,'col_q'=4,'col_b'=2] {'col_..., dimensions={0} | all-to-all | bytes 786432 | tf_op jit(solution)/shard_map/all_to_all | solution.py:369
  159.0 1.3 shard_map.117
  160.3 12.8 %all_to_all.62.got_ref = bf16[64,2,576]{2,1,0:T(2,128)(2,1)S(1)} all-to-all(bf16[64,2,576]{2,1,0:T(2,128)(2,1)S(1)} %get-tuple-element.54), channel_id=1, replica_groups=mesh['row_a'=2,'row_q'=4,'row_b'=2,'col_a'=2,'col_q'=4,'col_b'=2] {'col_..., dimensions={0} | all-to-all | bytes 294912 | tf_op jit(solution)/shard_map/all_to_all | solution.py:369
  173.1 1.3 shard_map.118
  174.4 8.9 %all_to_all.63.got_ref = bf16[16,32,128]{2,1,0:T(8,128)(2,1)S(1)} all-to-all(bf16[16,32,128]{2,1,0:T(8,128)(2,1)S(1)} %bitcast.7), channel_id=1, replica_groups=mesh['row_a'=2,'row_q'=4,'row_b'=2,'col_a'=2,'col_q'=4,'col_b'=2] {'row_..., dimensions={0} | all-to-all | bytes 262144 | tf_op jit(solution)/shard_map/all_to_all | solution.py:369
  183.4 13.0 %all_to_all.64.got_ref = bf16[16,40,128]{2,1,0:T(8,128)(2,1)S(1)} all-to-all(bf16[16,40,128]{2,1,0:T(8,128)(2,1)S(1)} %shard_map.119), channel_id=1, replica_groups=mesh['row_a'=2,'row_q'=4,'row_b'=2,'col_a'=2,'col_q'=4,'col_b'=2] {'col_..., dimensions={0} | all-to-all | bytes 327680 | tf_op jit(solution)/shard_map/all_to_all | solution.py:369
  196.5 11.8 %all_to_all.65.got_ref = bf16[16,64,128]{2,1,0:T(8,128)(2,1)S(1)} all-to-all(bf16[16,64,128]{2,1,0:T(8,128)(2,1)S(1)} %shard_map.120), channel_id=1, replica_groups=mesh['row_a'=2,'row_q'=4,'row_b'=2,'col_a'=2,'col_q'=4,'col_b'=2] {'row_..., dimensions={0} | all-to-all | bytes 524288 | tf_op jit(solution)/shard_map/all_to_all | solution.py:369
  208.2 0.9 shard_map.121
  (2 shorter events, 0.1 us)
Async XLA Ops:
  0.6 1.0 copy-start.3
  1.6 0.9 copy-start.2
  22.9 28.2 %copy-start.1 = (bf16[128,384]{1,0:T(8,128)(2,1)S(1)}, bf16[128,384]{1,0:T(8,128)(2,1)}, u32[]{:S(2)}) copy-start(bf16[128,384]{1,0:T(8,128)(2,1)} %w_in_ref.4) | copy-start | bytes 294916
  22.9 28.2 %copy-start.4 = (bf16[64,128]{1,0:T(8,128)(2,1)S(1)}, bf16[64,128]{1,0:T(8,128)(2,1)}, u32[]{:S(2)}) copy-start(bf16[64,128]{1,0:T(8,128)(2,1)} %w_out_ref.5) | copy-start | bytes 49156
  69.1 23.6 %copy-start = (f32[24,24,128]{2,1,0:T(8,128)S(1)}, f32[24,24,128]{2,1,0:T(8,128)}, u32[]{:S(2)}) copy-start(f32[24,24,128]{2,1,0:T(8,128)} %param.7) | copy-start | bytes 884740
  69.2 23.5 %copy-start.5 = (bf16[64,128]{1,0:T(8,128)(2,1)S(1)}, bf16[64,128]{1,0:T(8,128)(2,1)}, u32[]{:S(2)}) copy-start(bf16[64,128]{1,0:T(8,128)(2,1)} %w_out_ref.4) | copy-start | bytes 49156

commit v6 on v5

--- a/solution.py
+++ b/solution.py
@@ -301,7 +301,7 @@
         empty = jnp.zeros((refs[1].shape[0] - len(sums), sums[0].shape[1]), F32)
         refs[1][...] = jnp.concatenate(sums + [empty], axis=0).astype(BF16)
     got = jnp.concatenate([x[:, :half] for x in got], axis=1)
-    grad = blocks(got, size, wide, size, wide).astype(BF16)
+    grad = blocks_low(got.astype(BF16), size, wide, size, wide)
     sent = [blocks(dot(grad, second_ref[...], 1, 0), wide, part, size, wide)]
     scratch[...] = dot(grad, first_ref[...], 0, 0)
     sent.append(blocks(reorder(scratch, size, wide), wide, part, size, wide))

time: 210 us -> 209 us (level)
  no operation moved by 1% of the time
where the time goes in v6:
time: 209 us
  blocking collectives  196 us (94%)
  Pallas kernels  10.9 us (5%)
    all_to_all x11, blocking collectives, exchange(): return lax.all_to_all(x, axes, 0, 0, tiled=True)  196 us
    pallas_call x13, Pallas kernels, call(): pl.pallas_call(body, out_shape=[jax.ShapeDtypeStruct(s, t) for s, t in ou...  10.9 us

profile of v6, /device:TPU:1, one launch (start us, length us, event | category | flops | bytes accessed | tf_op | source)
XLA Modules:
  0.0 208.9 jit_solution(15736291491235176810)
XLA Ops:
  0.6 0.0 copy-start.3
  0.6 1.0 copy-done.3
  1.6 0.0 copy-start.2
  1.6 0.2 shard_map.109
  1.8 0.7 copy-done.2
  2.5 0.4 shard_map.110
  2.9 19.0 %all_to_all.55.got_ref = bf16[64,2,576]{2,1,0:T(2,128)(2,1)S(1)} all-to-all(bf16[64,2,576]{2,1,0:T(2,128)(2,1)S(1)} %get-tuple-element.37), channel_id=1, replica_groups=mesh['row_a'=2,'row_q'=4,'row_b'=2,'col_a'=2,'col_q'=4,'col_b'=2] {'col_..., dimensions={0} | all-to-all | bytes 294912 | tf_op jit(solution)/shard_map/all_to_all | solution.py:369
  21.8 1.1 shard_map.111
  22.9 0.0 copy-start.1
  22.9 0.0 copy-start.4
  23.0 28.2 %all_to_all.56.got_ref = bf16[256,2,288]{2,1,0:T(2,128)(2,1)S(1)} all-to-all(bf16[256,2,288]{2,1,0:T(2,128)(2,1)S(1)} %get-tuple-element.38), channel_id=1, replica_groups=mesh['row_a'=2,'row_q'=4,'row_b'=2,'col_a'=2,'col_q'=4,'col_b'=2] {'col_..., dimensions={0} | all-to-all | bytes 589824 | tf_op jit(solution)/shard_map/all_to_all | solution.py:369
  51.2 0.0 copy-done.1
  51.2 0.0 copy-done.4
  51.2 1.0 shard_map.112
  52.2 15.9 %all_to_all.57.got_ref = bf16[64,2,576]{2,1,0:T(2,128)(2,1)S(1)} all-to-all(bf16[64,2,576]{2,1,0:T(2,128)(2,1)S(1)} %get-tuple-element.41), channel_id=1, replica_groups=mesh['row_a'=2,'row_q'=4,'row_b'=2,'col_a'=2,'col_q'=4,'col_b'=2] {'row_..., dimensions={0} | all-to-all | bytes 294912 | tf_op jit(solution)/shard_map/all_to_all | solution.py:369
  68.0 1.1 shard_map.113
  69.1 0.0 copy-start
  69.2 0.0 copy-start.5
  69.2 23.5 %all_to_all.58.got_ref = bf16[256,2,288]{2,1,0:T(2,128)(2,1)S(1)} all-to-all(bf16[256,2,288]{2,1,0:T(2,128)(2,1)S(1)} %get-tuple-element.42), channel_id=1, replica_groups=mesh['row_a'=2,'row_q'=4,'row_b'=2,'col_a'=2,'col_q'=4,'col_b'=2] {'row_..., dimensions={0} | all-to-all | bytes 589824 | tf_op jit(solution)/shard_map/all_to_all | solution.py:369
  92.7 0.0 copy-done
  92.7 0.0 copy-done.5
  92.7 1.2 shard_map.114
  93.9 23.8 %all_to_all.59.got_ref = bf16[256,2,288]{2,1,0:T(2,128)(2,1)S(1)} all-to-all(bf16[256,2,288]{2,1,0:T(2,128)(2,1)S(1)} %get-tuple-element.46), channel_id=1, replica_groups=mesh['row_a'=2,'row_q'=4,'row_b'=2,'col_a'=2,'col_q'=4,'col_b'=2] {'row_..., dimensions={0} | all-to-all | bytes 589824 | tf_op jit(solution)/shard_map/all_to_all | solution.py:369
  117.8 1.1 shard_map.115
  118.8 15.5 %all_to_all.60.got_ref = bf16[64,2,576]{2,1,0:T(2,128)(2,1)S(1)} all-to-all(bf16[64,2,576]{2,1,0:T(2,128)(2,1)S(1)} %shard_map.115), channel_id=1, replica_groups=mesh['row_a'=2,'row_q'=4,'row_b'=2,'col_a'=2,'col_q'=4,'col_b'=2] {'row_..., dimensions={0} | all-to-all | bytes 294912 | tf_op jit(solution)/shard_map/all_to_all | solution.py:369
  134.3 1.4 shard_map.116
  135.7 23.1 %all_to_all.61.got_ref = bf16[256,2,384]{2,1,0:T(2,128)(2,1)S(1)} all-to-all(bf16[256,2,384]{2,1,0:T(2,128)(2,1)S(1)} %get-tuple-element.51), channel_id=1, replica_groups=mesh['row_a'=2,'row_q'=4,'row_b'=2,'col_a'=2,'col_q'=4,'col_b'=2] {'col_..., dimensions={0} | all-to-all | bytes 786432 | tf_op jit(solution)/shard_map/all_to_all | solution.py:369
  158.9 1.1 shard_map.117
  160.0 12.8 %all_to_all.62.got_ref = bf16[64,2,576]{2,1,0:T(2,128)(2,1)S(1)} all-to-all(bf16[64,2,576]{2,1,0:T(2,128)(2,1)S(1)} %get-tuple-element.54), channel_id=1, replica_groups=mesh['row_a'=2,'row_q'=4,'row_b'=2,'col_a'=2,'col_q'=4,'col_b'=2] {'col_..., dimensions={0} | all-to-all | bytes 294912 | tf_op jit(solution)/shard_map/all_to_all | solution.py:369
  172.8 1.3 shard_map.118
  174.1 8.9 %all_to_all.63.got_ref = bf16[16,32,128]{2,1,0:T(8,128)(2,1)S(1)} all-to-all(bf16[16,32,128]{2,1,0:T(8,128)(2,1)S(1)} %bitcast.7), channel_id=1, replica_groups=mesh['row_a'=2,'row_q'=4,'row_b'=2,'col_a'=2,'col_q'=4,'col_b'=2] {'row_..., dimensions={0} | all-to-all | bytes 262144 | tf_op jit(solution)/shard_map/all_to_all | solution.py:369
  183.1 13.0 %all_to_all.64.got_ref = bf16[16,40,128]{2,1,0:T(8,128)(2,1)S(1)} all-to-all(bf16[16,40,128]{2,1,0:T(8,128)(2,1)S(1)} %shard_map.119), channel_id=1, replica_groups=mesh['row_a'=2,'row_q'=4,'row_b'=2,'col_a'=2,'col_q'=4,'col_b'=2] {'col_..., dimensions={0} | all-to-all | bytes 327680 | tf_op jit(solution)/shard_map/all_to_all | solution.py:369
  196.2 11.8 %all_to_all.65.got_ref = bf16[16,64,128]{2,1,0:T(8,128)(2,1)S(1)} all-to-all(bf16[16,64,128]{2,1,0:T(8,128)(2,1)S(1)} %shard_map.120), channel_id=1, replica_groups=mesh['row_a'=2,'row_q'=4,'row_b'=2,'col_a'=2,'col_q'=4,'col_b'=2] {'row_..., dimensions={0} | all-to-all | bytes 524288 | tf_op jit(solution)/shard_map/all_to_all | solution.py:369
  207.9 0.9 shard_map.121
  (2 shorter events, 0.1 us)
Async XLA Ops:
  0.6 1.0 copy-start.3
  1.6 0.9 copy-start.2
  22.9 28.2 %copy-start.1 = (bf16[128,384]{1,0:T(8,128)(2,1)S(1)}, bf16[128,384]{1,0:T(8,128)(2,1)}, u32[]{:S(2)}) copy-start(bf16[128,384]{1,0:T(8,128)(2,1)} %w_in_ref.4) | copy-start | bytes 294916
  22.9 28.2 %copy-start.4 = (bf16[64,128]{1,0:T(8,128)(2,1)S(1)}, bf16[64,128]{1,0:T(8,128)(2,1)}, u32[]{:S(2)}) copy-start(bf16[64,128]{1,0:T(8,128)(2,1)} %w_out_ref.5) | copy-start | bytes 49156
  69.1 23.6 %copy-start = (f32[24,24,128]{2,1,0:T(8,128)S(1)}, f32[24,24,128]{2,1,0:T(8,128)}, u32[]{:S(2)}) copy-start(f32[24,24,128]{2,1,0:T(8,128)} %param.7) | copy-start | bytes 884740
  69.2 23.5 %copy-start.5 = (bf16[64,128]{1,0:T(8,128)(2,1)S(1)}, bf16[64,128]{1,0:T(8,128)(2,1)}, u32[]{:S(2)}) copy-start(bf16[64,128]{1,0:T(8,128)(2,1)} %w_out_ref.4) | copy-start | bytes 49156

commit v7 on v6

--- a/solution.py
+++ b/solution.py
@@ -118,27 +118,31 @@
     return norm_back(dot(w_out, grad_proj, 1, 0), normed, rstd), grad_gate, grad_w
 
 
-def owners(count, h):
-    run = h // SPLIT
-    return [(at, (at // run // PARTS) * run, run) for at in range(0, count, run)]
-
-
-def summed(got_ref):
+def owners(count, h, outer_first=True):
+    run = h // (SPLIT * SPLIT)
+    found = []
+    for at in range(0, count, run):
+        a, b = at // (run * SPLIT * PARTS), at // run % SPLIT
+        found.append((at, (a * SPLIT + b if outer_first else b * SPLIT + a) * run, run))
+    return found
+
+
+def summed(got_ref, outer_first=True):
     count = got_ref.shape[0]
     h = count // PARTS
     def total(k):
         sums = {}
-        for at, channel, run in owners(count, h):
+        for at, channel, run in owners(count, h, outer_first):
             part = got_ref[at : at + run, k, :].astype(F32)
             sums[channel] = sums[channel] + part if channel in sums else part
-        return jnp.concatenate(list(sums.values()), axis=0)
+        return jnp.concatenate([sums[channel] for channel in sorted(sums)], axis=0)
 
     return jnp.concatenate([total(0), total(1)], axis=1)
 
 
-def to_owners(x):
+def to_owners(x, outer_first=True):
     h, cells = x.shape
-    runs = [x[channel : channel + run] for _, channel, run in owners(PARTS * h, h)]
+    runs = [x[channel : channel + run] for _, channel, run in owners(PARTS * h, h, outer_first)]
     x = jnp.concatenate(runs, axis=0)
     return [x[:, : cells // 2], x[:, cells // 2 :]]
 
@@ -158,7 +162,7 @@
     sent_ref, proj2_ref, mixed_ref, mid_ref, scratch, pairs_out,
 ):
     h = sent_ref.shape[0]
-    mixed = summed(got_ref)
+    mixed = summed(got_ref, False)
     mixed_ref[...] = mixed
     out, *_ = finish(mixed, w_out_ref[...])
     mid = pair_t_ref[...] + jax.nn.sigmoid(proj1_ref[4 * h :, :]) * out
@@ -212,7 +216,7 @@
         jnp.concatenate(
             [x, jnp.concatenate([w[k * pairs : (k + 1) * pairs] for w in weights], axis=0)], axis=1
         )
-        for k, x in enumerate(to_owners(grad))
+        for k, x in enumerate(to_owners(grad, False))
     ]
     write_plain(sent_ref, sent)
 
@@ -400,7 +404,7 @@
         )
         return (exchange(sent, group), *rest)
 
-    one = (("col_a", "col_b") + ROW, COL + ROW)
+    one = (("col_b", "col_a") + ROW, COL + ROW)
     two = (("row_a", "row_b") + COL, ROW + COL)
     slice_wide = wide * c // (2 * size * size)
 

time: 209 us -> 209 us (level)
  no operation moved by 1% of the time
where the time goes in v7:
time: 209 us
  blocking collectives  195 us (93%)
  Pallas kernels  10.9 us (5%)
    all_to_all x11, blocking collectives, exchange(): return lax.all_to_all(x, axes, 0, 0, tiled=True)  195 us
    pallas_call x13, Pallas kernels, call(): pl.pallas_call(body, out_shape=[jax.ShapeDtypeStruct(s, t) for s, t in ou...  10.9 us

profile of v7, /device:TPU:1, one launch (start us, length us, event | category | flops | bytes accessed | tf_op | source)
XLA Modules:
  0.0 208.7 jit_solution(10071600334355933503)
XLA Ops:
  0.6 0.0 copy-start.3
  0.6 1.0 copy-done.3
  1.6 0.0 copy-start.2
  1.6 0.2 shard_map.109
  1.8 0.7 copy-done.2
  2.5 0.4 shard_map.110
  2.9 19.0 %all_to_all.55.got_ref = bf16[64,2,576]{2,1,0:T(2,128)(2,1)S(1)} all-to-all(bf16[64,2,576]{2,1,0:T(2,128)(2,1)S(1)} %get-tuple-element.37), channel_id=1, replica_groups=mesh['row_a'=2,'row_q'=4,'row_b'=2,'col_a'=2,'col_q'=4,'col_b'=2] {'col_..., dimensions={0} | all-to-all | bytes 294912 | tf_op jit(solution)/shard_map/all_to_all | solution.py:373
  21.8 1.1 shard_map.111
  22.9 0.0 copy-start.1
  22.9 0.0 copy-start.4
  23.0 28.0 %all_to_all.56.got_ref = bf16[256,2,288]{2,1,0:T(2,128)(2,1)S(1)} all-to-all(bf16[256,2,288]{2,1,0:T(2,128)(2,1)S(1)} %get-tuple-element.38), channel_id=1, replica_groups=mesh['row_a'=2,'row_q'=4,'row_b'=2,'col_a'=2,'col_q'=4,'col_b'=2] {'col_..., dimensions={0} | all-to-all | bytes 589824 | tf_op jit(solution)/shard_map/all_to_all | solution.py:373
  51.0 0.0 copy-done.1
  51.0 0.0 copy-done.4
  51.0 1.0 shard_map.112
  51.9 15.9 %all_to_all.57.got_ref = bf16[64,2,576]{2,1,0:T(2,128)(2,1)S(1)} all-to-all(bf16[64,2,576]{2,1,0:T(2,128)(2,1)S(1)} %get-tuple-element.41), channel_id=1, replica_groups=mesh['row_a'=2,'row_q'=4,'row_b'=2,'col_a'=2,'col_q'=4,'col_b'=2] {'row_..., dimensions={0} | all-to-all | bytes 294912 | tf_op jit(solution)/shard_map/all_to_all | solution.py:373
  67.8 1.1 shard_map.113
  68.9 0.0 copy-start
  68.9 0.0 copy-start.5
  68.9 23.5 %all_to_all.58.got_ref = bf16[256,2,288]{2,1,0:T(2,128)(2,1)S(1)} all-to-all(bf16[256,2,288]{2,1,0:T(2,128)(2,1)S(1)} %get-tuple-element.42), channel_id=1, replica_groups=mesh['row_a'=2,'row_q'=4,'row_b'=2,'col_a'=2,'col_q'=4,'col_b'=2] {'row_..., dimensions={0} | all-to-all | bytes 589824 | tf_op jit(solution)/shard_map/all_to_all | solution.py:373
  92.5 0.0 copy-done
  92.5 0.0 copy-done.5
  92.5 1.2 shard_map.114
  93.7 23.8 %all_to_all.59.got_ref = bf16[256,2,288]{2,1,0:T(2,128)(2,1)S(1)} all-to-all(bf16[256,2,288]{2,1,0:T(2,128)(2,1)S(1)} %get-tuple-element.46), channel_id=1, replica_groups=mesh['row_a'=2,'row_q'=4,'row_b'=2,'col_a'=2,'col_q'=4,'col_b'=2] {'row_..., dimensions={0} | all-to-all | bytes 589824 | tf_op jit(solution)/shard_map/all_to_all | solution.py:373
  117.5 1.1 shard_map.115
  118.6 15.5 %all_to_all.60.got_ref = bf16[64,2,576]{2,1,0:T(2,128)(2,1)S(1)} all-to-all(bf16[64,2,576]{2,1,0:T(2,128)(2,1)S(1)} %shard_map.115), channel_id=1, replica_groups=mesh['row_a'=2,'row_q'=4,'row_b'=2,'col_a'=2,'col_q'=4,'col_b'=2] {'row_..., dimensions={0} | all-to-all | bytes 294912 | tf_op jit(solution)/shard_map/all_to_all | solution.py:373
  134.1 1.4 shard_map.116
  135.5 23.1 %all_to_all.61.got_ref = bf16[256,2,384]{2,1,0:T(2,128)(2,1)S(1)} all-to-all(bf16[256,2,384]{2,1,0:T(2,128)(2,1)S(1)} %get-tuple-element.51), channel_id=1, replica_groups=mesh['row_a'=2,'row_q'=4,'row_b'=2,'col_a'=2,'col_q'=4,'col_b'=2] {'col_..., dimensions={0} | all-to-all | bytes 786432 | tf_op jit(solution)/shard_map/all_to_all | solution.py:373
  158.7 1.1 shard_map.117
  159.8 12.8 %all_to_all.62.got_ref = bf16[64,2,576]{2,1,0:T(2,128)(2,1)S(1)} all-to-all(bf16[64,2,576]{2,1,0:T(2,128)(2,1)S(1)} %get-tuple-element.54), channel_id=1, replica_groups=mesh['row_a'=2,'row_q'=4,'row_b'=2,'col_a'=2,'col_q'=4,'col_b'=2] {'col_..., dimensions={0} | all-to-all | bytes 294912 | tf_op jit(solution)/shard_map/all_to_all | solution.py:373
  172.6 1.3 shard_map.118
  173.9 8.9 %all_to_all.63.got_ref = bf16[16,32,128]{2,1,0:T(8,128)(2,1)S(1)} all-to-all(bf16[16,32,128]{2,1,0:T(8,128)(2,1)S(1)} %bitcast.7), channel_id=1, replica_groups=mesh['row_a'=2,'row_q'=4,'row_b'=2,'col_a'=2,'col_q'=4,'col_b'=2] {'row_..., dimensions={0} | all-to-all | bytes 262144 | tf_op jit(solution)/shard_map/all_to_all | solution.py:373
  182.9 13.0 %all_to_all.64.got_ref = bf16[16,40,128]{2,1,0:T(8,128)(2,1)S(1)} all-to-all(bf16[16,40,128]{2,1,0:T(8,128)(2,1)S(1)} %shard_map.119), channel_id=1, replica_groups=mesh['row_a'=2,'row_q'=4,'row_b'=2,'col_a'=2,'col_q'=4,'col_b'=2] {'col_..., dimensions={0} | all-to-all | bytes 327680 | tf_op jit(solution)/shard_map/all_to_all | solution.py:373
  196.0 11.8 %all_to_all.65.got_ref = bf16[16,64,128]{2,1,0:T(8,128)(2,1)S(1)} all-to-all(bf16[16,64,128]{2,1,0:T(8,128)(2,1)S(1)} %shard_map.120), channel_id=1, replica_groups=mesh['row_a'=2,'row_q'=4,'row_b'=2,'col_a'=2,'col_q'=4,'col_b'=2] {'row_..., dimensions={0} | all-to-all | bytes 524288 | tf_op jit(solution)/shard_map/all_to_all | solution.py:373
  207.7 0.9 shard_map.121
  (2 shorter events, 0.1 us)
Async XLA Ops:
  0.6 1.0 copy-start.3
  1.6 0.9 copy-start.2
  22.9 28.0 %copy-start.1 = (bf16[128,384]{1,0:T(8,128)(2,1)S(1)}, bf16[128,384]{1,0:T(8,128)(2,1)}, u32[]{:S(2)}) copy-start(bf16[128,384]{1,0:T(8,128)(2,1)} %w_in_ref.4) | copy-start | bytes 294916
  22.9 28.0 %copy-start.4 = (bf16[64,128]{1,0:T(8,128)(2,1)S(1)}, bf16[64,128]{1,0:T(8,128)(2,1)}, u32[]{:S(2)}) copy-start(bf16[64,128]{1,0:T(8,128)(2,1)} %w_out_ref.5) | copy-start | bytes 49156
  68.9 23.6 %copy-start = (f32[24,24,128]{2,1,0:T(8,128)S(1)}, f32[24,24,128]{2,1,0:T(8,128)}, u32[]{:S(2)}) copy-start(f32[24,24,128]{2,1,0:T(8,128)} %param.7) | copy-start | bytes 884740
  68.9 23.5 %copy-start.5 = (bf16[64,128]{1,0:T(8,128)(2,1)S(1)}, bf16[64,128]{1,0:T(8,128)(2,1)}, u32[]{:S(2)}) copy-start(bf16[64,128]{1,0:T(8,128)(2,1)} %w_out_ref.4) | copy-start | bytes 49156

commit v8 on v7

--- a/solution.py
+++ b/solution.py
@@ -178,14 +178,14 @@
 ):
     h = got_ref.shape[0] // PARTS
     n = new_ref.shape[0]
-    out, normed, rstd, post = finish(summed(got_ref), w_out_ref[...])
+    out, normed, rstd, post = finish(summed(got_ref, False), w_out_ref[...])
     gate = jax.nn.sigmoid(proj_ref[4 * h :, :])
     new = (mid_ref[...] + gate * out).T
     scratch[...] = new
     new_ref[...] = swap_cells(scratch, n).reshape(new_ref.shape)
     grad_new = swap_cells(grad_out_ref, n).T
     grad, grad_gate, grad_w = finish_back(grad_new, gate, out, normed, rstd, post, w_out_ref[...])
-    write_plain(sent_ref, to_owners(grad))
+    write_plain(sent_ref, to_owners(grad, False))
     grad_gate_ref[...] = grad_gate
     grad_w_ref[...] = grad_w
 
@@ -405,7 +405,7 @@
         return (exchange(sent, group), *rest)
 
     one = (("col_b", "col_a") + ROW, COL + ROW)
-    two = (("row_a", "row_b") + COL, ROW + COL)
+    two = (("row_b", "row_a") + COL, ROW + COL)
     slice_wide = wide * c // (2 * size * size)
 
     pair_t, normed1 = call(turn_pair, [cell_array, ((c, cells), BF16)], pair)

time: 209 us -> 209 us (level)
  no operation moved by 1% of the time
where the time goes in v8:
time: 209 us
  blocking collectives  195 us (93%)
  Pallas kernels  11 us (5%)
    all_to_all x11, blocking collectives, exchange(): return lax.all_to_all(x, axes, 0, 0, tiled=True)  195 us
    pallas_call x13, Pallas kernels, call(): pl.pallas_call(body, out_shape=[jax.ShapeDtypeStruct(s, t) for s, t in ou...  11 us

profile of v8, /device:TPU:1, one launch (start us, length us, event | category | flops | bytes accessed | tf_op | source)
XLA Modules:
  0.0 208.8 jit_solution(8965405948343265144)
XLA Ops:
  0.6 0.0 copy-start.3
  0.6 1.0 copy-done.3
  1.6 0.0 copy-start.2
  1.6 0.2 shard_map.109
  1.8 0.7 copy-done.2
  2.5 0.4 shard_map.110
  2.9 19.0 %all_to_all.55.got_ref = bf16[64,2,576]{2,1,0:T(2,128)(2,1)S(1)} all-to-all(bf16[64,2,576]{2,1,0:T(2,128)(2,1)S(1)} %get-tuple-element.37), channel_id=1, replica_groups=mesh['row_a'=2,'row_q'=4,'row_b'=2,'col_a'=2,'col_q'=4,'col_b'=2] {'col_..., dimensions={0} | all-to-all | bytes 294912 | tf_op jit(solution)/shard_map/all_to_all | solution.py:373
  21.8 1.1 shard_map.111
  22.9 0.0 copy-start.1
  22.9 0.0 copy-start.4
  23.0 28.0 %all_to_all.56.got_ref = bf16[256,2,288]{2,1,0:T(2,128)(2,1)S(1)} all-to-all(bf16[256,2,288]{2,1,0:T(2,128)(2,1)S(1)} %get-tuple-element.38), channel_id=1, replica_groups=mesh['row_a'=2,'row_q'=4,'row_b'=2,'col_a'=2,'col_q'=4,'col_b'=2] {'col_..., dimensions={0} | all-to-all | bytes 589824 | tf_op jit(solution)/shard_map/all_to_all | solution.py:373
  51.0 0.0 copy-done.1
  51.0 0.0 copy-done.4
  51.0 1.0 shard_map.112
  51.9 15.8 %all_to_all.57.got_ref = bf16[64,2,576]{2,1,0:T(2,128)(2,1)S(1)} all-to-all(bf16[64,2,576]{2,1,0:T(2,128)(2,1)S(1)} %get-tuple-element.41), channel_id=1, replica_groups=mesh['row_a'=2,'row_q'=4,'row_b'=2,'col_a'=2,'col_q'=4,'col_b'=2] {'row_..., dimensions={0} | all-to-all | bytes 294912 | tf_op jit(solution)/shard_map/all_to_all | solution.py:373
  67.8 1.1 shard_map.113
  68.9 0.0 copy-start
  68.9 0.0 copy-start.5
  68.9 23.6 %all_to_all.58.got_ref = bf16[256,2,288]{2,1,0:T(2,128)(2,1)S(1)} all-to-all(bf16[256,2,288]{2,1,0:T(2,128)(2,1)S(1)} %get-tuple-element.42), channel_id=1, replica_groups=mesh['row_a'=2,'row_q'=4,'row_b'=2,'col_a'=2,'col_q'=4,'col_b'=2] {'row_..., dimensions={0} | all-to-all | bytes 589824 | tf_op jit(solution)/shard_map/all_to_all | solution.py:373
  92.5 0.0 copy-done
  92.5 0.0 copy-done.5
  92.5 1.3 shard_map.114
  93.8 23.8 %all_to_all.59.got_ref = bf16[256,2,288]{2,1,0:T(2,128)(2,1)S(1)} all-to-all(bf16[256,2,288]{2,1,0:T(2,128)(2,1)S(1)} %get-tuple-element.46), channel_id=1, replica_groups=mesh['row_a'=2,'row_q'=4,'row_b'=2,'col_a'=2,'col_q'=4,'col_b'=2] {'row_..., dimensions={0} | all-to-all | bytes 589824 | tf_op jit(solution)/shard_map/all_to_all | solution.py:373
  117.6 1.1 shard_map.115
  118.7 15.5 %all_to_all.60.got_ref = bf16[64,2,576]{2,1,0:T(2,128)(2,1)S(1)} all-to-all(bf16[64,2,576]{2,1,0:T(2,128)(2,1)S(1)} %shard_map.115), channel_id=1, replica_groups=mesh['row_a'=2,'row_q'=4,'row_b'=2,'col_a'=2,'col_q'=4,'col_b'=2] {'row_..., dimensions={0} | all-to-all | bytes 294912 | tf_op jit(solution)/shard_map/all_to_all | solution.py:373
  134.2 1.4 shard_map.116
  135.6 23.2 %all_to_all.61.got_ref = bf16[256,2,384]{2,1,0:T(2,128)(2,1)S(1)} all-to-all(bf16[256,2,384]{2,1,0:T(2,128)(2,1)S(1)} %get-tuple-element.51), channel_id=1, replica_groups=mesh['row_a'=2,'row_q'=4,'row_b'=2,'col_a'=2,'col_q'=4,'col_b'=2] {'col_..., dimensions={0} | all-to-all | bytes 786432 | tf_op jit(solution)/shard_map/all_to_all | solution.py:373
  158.8 1.1 shard_map.117
  159.9 12.8 %all_to_all.62.got_ref = bf16[64,2,576]{2,1,0:T(2,128)(2,1)S(1)} all-to-all(bf16[64,2,576]{2,1,0:T(2,128)(2,1)S(1)} %get-tuple-element.54), channel_id=1, replica_groups=mesh['row_a'=2,'row_q'=4,'row_b'=2,'col_a'=2,'col_q'=4,'col_b'=2] {'col_..., dimensions={0} | all-to-all | bytes 294912 | tf_op jit(solution)/shard_map/all_to_all | solution.py:373
  172.7 1.3 shard_map.118
  174.0 8.9 %all_to_all.63.got_ref = bf16[16,32,128]{2,1,0:T(8,128)(2,1)S(1)} all-to-all(bf16[16,32,128]{2,1,0:T(8,128)(2,1)S(1)} %bitcast.7), channel_id=1, replica_groups=mesh['row_a'=2,'row_q'=4,'row_b'=2,'col_a'=2,'col_q'=4,'col_b'=2] {'row_..., dimensions={0} | all-to-all | bytes 262144 | tf_op jit(solution)/shard_map/all_to_all | solution.py:373
  183.0 13.0 %all_to_all.64.got_ref = bf16[16,40,128]{2,1,0:T(8,128)(2,1)S(1)} all-to-all(bf16[16,40,128]{2,1,0:T(8,128)(2,1)S(1)} %shard_map.119), channel_id=1, replica_groups=mesh['row_a'=2,'row_q'=4,'row_b'=2,'col_a'=2,'col_q'=4,'col_b'=2] {'col_..., dimensions={0} | all-to-all | bytes 327680 | tf_op jit(solution)/shard_map/all_to_all | solution.py:373
  196.1 11.8 %all_to_all.65.got_ref = bf16[16,64,128]{2,1,0:T(8,128)(2,1)S(1)} all-to-all(bf16[16,64,128]{2,1,0:T(8,128)(2,1)S(1)} %shard_map.120), channel_id=1, replica_groups=mesh['row_a'=2,'row_q'=4,'row_b'=2,'col_a'=2,'col_q'=4,'col_b'=2] {'row_..., dimensions={0} | all-to-all | bytes 524288 | tf_op jit(solution)/shard_map/all_to_all | solution.py:373
  207.8 0.9 shard_map.121
  (2 shorter events, 0.1 us)
Async XLA Ops:
  0.6 1.0 copy-start.3
  1.6 0.9 copy-start.2
  22.9 28.0 %copy-start.1 = (bf16[128,384]{1,0:T(8,128)(2,1)S(1)}, bf16[128,384]{1,0:T(8,128)(2,1)}, u32[]{:S(2)}) copy-start(bf16[128,384]{1,0:T(8,128)(2,1)} %w_in_ref.4) | copy-start | bytes 294916
  22.9 28.0 %copy-start.4 = (bf16[64,128]{1,0:T(8,128)(2,1)S(1)}, bf16[64,128]{1,0:T(8,128)(2,1)}, u32[]{:S(2)}) copy-start(bf16[64,128]{1,0:T(8,128)(2,1)} %w_out_ref.5) | copy-start | bytes 49156
  68.9 23.6 %copy-start = (f32[24,24,128]{2,1,0:T(8,128)S(1)}, f32[24,24,128]{2,1,0:T(8,128)}, u32[]{:S(2)}) copy-start(f32[24,24,128]{2,1,0:T(8,128)} %param.7) | copy-start | bytes 884740
  68.9 23.6 %copy-start.5 = (bf16[64,128]{1,0:T(8,128)(2,1)S(1)}, bf16[64,128]{1,0:T(8,128)(2,1)}, u32[]{:S(2)}) copy-start(bf16[64,128]{1,0:T(8,128)(2,1)} %w_out_ref.4) | copy-start | bytes 49156
